TPU v7x, 256 devices: a whole 4x4x8 slice. The times are simulated.
256 devices in a mesh: row: 8 (over x_lo, y), col: 32 (over z, x_hi, core).
Axes of the slice: x: 4 (x_hi: 2, x_lo: 2; x = x_hi * 2 + x_lo), y: 4, z: 8, core: 2. Of those that a mesh axis runs over, the one named last changes fastest.
Arguments:
- hidden: bfloat16 [1024, 26624], P('col', 'row'), may hold values from -0.1875 to 0.1875
- grad_out: bfloat16 [1024, 16384], P('row', 'col'), may hold values from -6 to 6
- down_weight: bfloat16 [26624, 16384], P('row', 'col'), may hold values from -0.046875 to 0.046875
Outputs:
- weight_grad: bfloat16 [26624, 16384], P('row', 'col')
- hidden_grad: bfloat16 [1024, 26624], P('col', 'row')
All inputs are finite; a program needn't handle non-finite values.
Results may differ from a plain program's by a relative error of at most 0.001.
Values may be sent and summed in bfloat16 or wider, within the bound.
No kernel may reach another device: no remote copies, remote signals or barrier semaphores. Data moves between devices by JAX's collectives and lax.ppermute only.
A program may use at most 128 MiB of HBM per device.

v0:
```python
import jax
import jax.numpy as jnp
from jax import lax
from jax.sharding import PartitionSpec as P


def weight_part(hidden, grad_full):
    weight_sum = lax.dot_general(
        lax.all_gather(hidden, "col", axis=0, tiled=True),
        grad_full,
        (((0,), (0,)), ((), ())),
        preferred_element_type=jnp.float32,
    )
    return weight_sum.astype(jnp.bfloat16)


def input_part(grad_full, down_weight):
    return lax.psum_scatter(
        lax.dot_general(
            grad_full, down_weight, (((1,), (1,)), ((), ())), preferred_element_type=jnp.float32
        ),
        "col",
        scatter_dimension=0,
        tiled=True,
    ).astype(jnp.bfloat16)


def on_device(hidden, grad_out, down_weight):
    grad_full = lax.all_gather(grad_out, "row", axis=0, tiled=True)
    weight_grad = weight_part(hidden, grad_full)
    hidden_grad = input_part(grad_full, down_weight)
    return (weight_grad, hidden_grad)


def solution(mesh):
    in_specs = (P("col", "row"), P("row", "col"), P("row", "col"))
    out_specs = (P("row", "col"), P("col", "row"))
    return jax.shard_map(
        on_device, mesh=mesh, in_specs=in_specs, out_specs=out_specs, check_vma=False
    )
```

profile of v0, /device:TPU:1, one launch (start us, length us, event | category | flops | bytes accessed | tf_op | source)
XLA Modules:
  0.0 338.3 jit_solution(16728267841185608041)
XLA Ops:
  7.2 0.0 copy-start
  7.2 0.0 all-gather.5.cloned.1.call-start
  7.2 0.7 all-gather.5.cloned.1.call-update
  7.9 0.0 all-gather.3.cloned.1.call-start
  8.0 0.7 all-gather.3.cloned.1.call-update
  8.7 0.0 reduce-scatter.2.cloned.1.call-start
  8.7 41.5 %all-gather.5.cloned.1.call-done = bf16[1024,512]{1,0:T(8,128)(2,1)} async-done(((bf16[128,512]{1,0:T(8,128)(2,1)}), bf16[1024,512]{1,0:T(8,128)(2,1)}) %all-gather.5.cloned.1.call-update) | async-done | bytes 1048592 | tf_op jit(solution)/shard_map/all_gather | solution.py:29
  50.2 0.0 copy-done
  50.2 8.4 %fusion = f32[1024,3328]{1,0:T(8,128)} fusion(bf16[1024,512]{1,0:T(8,128)(2,1)} %all-gather.5.cloned.1.call-done, bf16[3328,512]{1,0:T(8,128)(2,1)S(1)} %copy-done), kind=kOutput, calls=%fused_computation.1 | convolution fusion | flops 3489660928 | bytes 18087936 | tf_op jit(solution)/shard_map/dot_general | solution.py:19
  58.6 0.0 reduce-scatter.2.cloned.1.call-update
  58.6 95.1 %all-gather.3.cloned.1.call-done = bf16[1024,3328]{1,0:T(8,128)(2,1)} async-done(((bf16[32,3328]{1,0:T(8,128)(2,1)}), bf16[1024,3328]{1,0:T(8,128)(2,1)}) %all-gather.3.cloned.1.call-update) | async-done | bytes 6815760 | tf_op jit(solution)/shard_map/all_gather | solution.py:9
  153.7 8.7 %convolution_convert_fusion = bf16[3328,512]{1,0:T(8,128)(2,1)} fusion(bf16[1024,3328]{1,0:T(8,128)(2,1)} %all-gather.3.cloned.1.call-done, bf16[1024,512]{1,0:T(8,128)(2,1)} %all-gather.5.cloned.1.call-done), kind=kOutput, calls=%fused_computation | convolution fusion | flops 3491364864 | bytes 11272192 | tf_op jit(solution)/shard_map/dot_general | solution.py:8
  162.4 167.7 %reduce-scatter.2.cloned.1.call-done = f32[32,3328]{1,0:T(8,128)} async-done(((f32[1024,3328]{1,0:T(8,128)}), f32[32,3328]{1,0:T(8,128)}) %reduce-scatter.2.cloned.1.call-update) | async-done | bytes 426000 | tf_op jit(solution)/shard_map/reduce_scatter | solution.py:18
  330.1 1.7 convert_element_type.7
Async XLA Ops:
  7.2 43.0 %copy-start = (bf16[3328,512]{1,0:T(8,128)(2,1)S(1)}, bf16[3328,512]{1,0:T(8,128)(2,1)}, u32[]{:S(2)}) copy-start(bf16[3328,512]{1,0:T(8,128)(2,1)} %param.5) | copy-start | bytes 10223620
  7.2 43.0 %all-gather.5.cloned.1.call-start = ((), (), s32[]{:S(2)}) async-start(), calls=%async_computation.2 | async-start | bytes 1179648 | tf_op jit(solution)/shard_map/all_gather | solution.py:29
  7.9 145.8 %all-gather.3.cloned.1.call-start = ((), (), s32[]{:S(2)}) async-start(), calls=%async_computation.1 | async-start | bytes 7028736 | tf_op jit(solution)/shard_map/all_gather | solution.py:9
  8.7 321.4 %reduce-scatter.2.cloned.1.call-start = ((), (), s32[]{:S(2)}) async-start(), calls=%async_computation.3 | async-start | bytes 14057472 | tf_op jit(solution)/shard_map/reduce_scatter | solution.py:18
Sparse Core Ops, SparseCore 0:
  9.8 40.3 all-gather.4
  53.0 100.7 all-gather.2
  158.3 171.7 reduce-scatter.1
where the time goes:
time: 341 us; the launch traced here: 338 us
  waiting for transfers between devices  306 us (90%)
  matrix products  17 us (5%)
  between operations  13.8 us (4%)
    reduce_scatter x1, waiting for transfers between devices, input_part(): lax.psum_scatter(lax.dot_general(grad_full, down_weight, (((1,), (1,)), (...  168 us
    all_gather x1, waiting for transfers between devices, weight_part(): lax.all_gather(hidden, 'col', axis=0, tiled=True)  95.1 us
    all_gather x1, waiting for transfers between devices, on_device(): grad_full = lax.all_gather(grad_out, 'row', axis=0, tiled=True)  41.5 us
    dot_general x1, matrix products, weight_part(): lax.dot_general(lax.all_gather(hidden, 'col', axis=0, tiled=True), grad_f...  8.66 us
    dot_general x1, matrix products, input_part(): lax.dot_general(grad_full, down_weight, (((1,), (1,)), ((), ())), preferr...  8.37 us
  transfers between devices with their start and end apart: 3, of which 3 were waited for; matrix products, arithmetic and copies ran while one was open for 5% of the time, Pallas kernels for 0%

commit v1 on v0

v1 whole, which is shorter than its diff:
```python
import functools

import jax
import jax.numpy as jnp
from jax import lax
from jax.experimental import pallas as pl
from jax.experimental.pallas import tpu as pltpu
from jax.sharding import PartitionSpec as P

ROWS, COLS, Z = 8, 32, 8
CHUNKS, PARTS, TIED, MARK, PACK = 1, 2, 2, 3, 40
F32, BF16 = jnp.float32, jnp.bfloat16
ANY = pl.BlockSpec(memory_space=pl.ANY)
HBM = pl.BlockSpec(memory_space=pltpu.HBM)
SMEM = pl.BlockSpec(memory_space=pltpu.SMEM)
VMEM = pl.BlockSpec(memory_space=pltpu.VMEM)


def col_flip(value, bits):
    return lax.ppermute(value, "col", [(c, c ^ bits) for c in range(COLS)])


def row_flip(value, bits):
    return lax.ppermute(value, "row", [(r, r ^ bits) for r in range(ROWS)])


def both_flip(value, row_bits, col_bits):
    pairs = [
        (r * COLS + c, (r ^ row_bits) * COLS + (c ^ col_bits))
        for r in range(ROWS)
        for c in range(COLS)
    ]
    return lax.ppermute(value, ("row", "col"), pairs)


def z_swap(value, side):
    def mate(z):
        return z ^ 1 if side == 0 else (z + 1 if z % 2 else z - 1) % Z

    return lax.ppermute(
        value, "col", [(c, mate(c // 4) * 4 + c % 4) for c in range(COLS)]
    )


Q, ZED, CORE, SIGN, X_HI = 8, 9, 10, 11, 12


def call(kernel, name, shapes, specs, args, out_specs=None, scratch=(), mib=8, flops=0, aliases={}):
    return pl.pallas_call(
        kernel,
        out_shape=[jax.ShapeDtypeStruct(shape, dtype) for shape, dtype in shapes],
        in_specs=specs,
        out_specs=out_specs or [VMEM] * len(shapes),
        scratch_shapes=list(scratch),
        compiler_params=pltpu.CompilerParams(vmem_limit_bytes=mib * 2**20),
        cost_estimate=pl.CostEstimate(
            flops=flops, bytes_accessed=2**20, transcendentals=0
        ),
        input_output_aliases=aliases,
        name=name,
    )(*args)


def weight_rows(where, down, out, sems, chunk, chunks):
    step = out.shape[0] // 2
    copies = []
    for core in range(2):
        at = (2 * (1 - where[X_HI]) + core) * (step * chunks) + chunk * step
        copies.append(
            pltpu.make_async_copy(
                down.at[pl.ds(pl.multiple_of(at, 16), step)],
                out.at[pl.ds(core * step, step)],
                sems.at[core],
            )
        )
        copies[-1].start()
    return copies


def pack_kernel(near, far, cross, own, out, sem):
    copy = pltpu.make_async_copy(own, out.at[0, 0], sem)
    copy.start()
    out[0, 1] = far[...]
    out[1, 0] = near[...]
    out[1, 1] = cross[...]
    copy.wait()


def order_kernel(where, piece, other, hidden, same, tokens, sem):
    x_hi = where[X_HI]
    copy = pltpu.make_async_copy(hidden, tokens.at[x_hi], sem)
    copy.start()
    tokens[1 - x_hi] = other[...]
    copy.wait()


def next_kernel(chunk, chunks, where, down, *refs):
    rows, sems = refs[-2:]
    for copy in weight_rows(where, down, rows, sems, chunk, chunks):
        copy.wait()


def gradient_rows(where, pieces, rows):
    for i, piece in enumerate(pieces):
        for a in range(2):
            block = where[2 * i + a]
            rows[block, :, :512] = piece[a, 0]
            rows[block, :, 512:] = piece[a, 1]


def feature_sum(chunk, chunks, where, down, got, rows, core, buf, sem, put):
    units = buf.shape[0]
    at = (2 * where[X_HI] + core) * (units * chunks) + chunk * units
    at = pl.multiple_of(at, 16)
    copy = pltpu.make_async_copy(down.at[pl.ds(at, units)], buf, sem)
    copy.start()
    copy.wait()
    inner = pl.multiple_of(core * units, 16)
    for pair in ((4, 3), (5, 2), (6, 1), (7, 0)):
        tokens = jnp.concatenate(
            [rows[lax.rem(where[ZED] + where[SIGN] * k + Z, Z)] for k in pair]
        )
        total = None
        for b, weights in enumerate((buf[...], got[pl.ds(inner, units), :])):
            part = lax.dot_general(
                weights,
                tokens[:, b * 512 : b * 512 + 512],
                (((1,), (1,)), ((), ())),
                preferred_element_type=F32,
            )
            total = part if total is None else total + part
        for i, k in enumerate(pair):
            put(k, total[:, i * 128 : i * 128 + 128])


FIRST, REST = (4, 3, 5), (2, 6, 1, 7, 0)


def rows_kernel(where, p0, p1, p2, p3, *refs):
    gradient_rows(where, (p0, p1, p2, p3), refs[-1])


def mate_kernel(chunk, chunks, where, down, got, rows, *refs):
    first, rest, buf, sem = refs[-4:]
    def put(k, value):
        if k in FIRST:
            first[FIRST.index(k)] = value
        else:
            rest[REST.index(k)] = value

    feature_sum(chunk, chunks, where, down, got, rows, 1 - where[CORE], buf, sem, put)


def own_kernel(chunk, chunks, where, down, got, rows, *refs):
    out, buf, sem = refs[-3:]

    def put(k, value):
        out[k] = value

    feature_sum(chunk, chunks, where, down, got, rows, where[CORE], buf, sem, put)


def part_of(part, size):
    return slice(part * size, part * size + size)


def send1_kernel(part, own, first, left, right):
    half = left.shape[0]
    lower, upper = part_of(2 * part, half), part_of(2 * part + 1, half)
    left[...] = own[4, lower] + first[0, lower]
    right[...] = own[4, upper] + first[0, upper]


def send2_kernel(part, own, first, came_left, came_right, left, right):
    half = came_left.shape[0]
    lower, upper = part_of(2 * part, half), part_of(2 * part + 1, half)
    left[:half] = own[3, lower] + first[1, lower]
    left[half:] = own[3, upper] + first[1, upper] + came_right[...]
    right[:half] = own[5, lower] + first[2, lower] + came_left[...]
    right[half:] = own[5, upper] + first[2, upper]


def send3_kernel(part, own, rest, came_left, came_right, left, right, near, far, base):
    at = part_of(part, left.shape[0])
    left[...] = own[2, at] + rest[0, at] + came_right[...]
    right[...] = own[6, at] + rest[1, at] + came_left[...]
    near[...] = own[1, at] + rest[2, at]
    far[...] = own[7, at] + rest[3, at]
    base[...] = own[0, at] + rest[4, at]


def send4_kernel(part, near, far, came_left, came_right, *refs):
    left, right = refs[-2:]
    left[...] = near[...] + came_right[...]
    right[...] = far[...] + came_left[...]


def last_kernel(*refs):
    out = refs[-1]
    for part in range(PARTS):
        base, came_left, came_right = refs[3 * part : 3 * part + 3]
        out[part_of(part, base.shape[0])] = base[...] + came_left[...] + came_right[...]


TILES = [(0, 512), (512, 512), (1024, 512), (1536, 512), (2048, 512), (2560, 768)]


def weight_kernel(where, rows, *refs):
    hiddens, out, mark = refs[:16], refs[16], refs[17]
    g_buf, o_buf, o_sem = refs[18:]
    row = 0
    for side in range(2):
        core = where[CORE] if side == 0 else 1 - where[CORE]
        for k in (0, 1, 2, 3, -1, -2, -3, 4):
            block = lax.rem(where[ZED] + k * where[SIGN] + Z, Z)
            for x_hi in range(2):
                at = pl.multiple_of(x_hi * 64 + core * 32, 32)
                g_buf[row : row + 32] = rows[block, pl.ds(at, 32), :512]
                row += 32
    stores = []
    for i, (at, size) in enumerate(TILES):
        lines = jnp.concatenate(
            [h[:, :, at : at + size].reshape(64, size) for h in hiddens], axis=0
        )
        o_buf[at : at + size] = lax.dot_general(
            lines, g_buf[...], (((0,), (0,)), ((), ())), preferred_element_type=F32
        ).astype(BF16)
        store = pltpu.make_async_copy(
            o_buf.at[pl.ds(at, size)], out.at[pl.ds(at, size)], o_sem.at[i]
        )
        store.start()
        stores.append(store)
    mark[...] = g_buf[:16, :128]
    for store in stores:
        store.wait()


def on_device(hidden, grad_out, down_weight):
    r, c = lax.axis_index("row"), lax.axis_index("col")
    z, q = c // 4, c % 4
    x_hi, core = q // 2, q % 2
    sign = 1 - 2 * (z % 2)
    width = down_weight.shape[0]
    units = width // 4
    where = jnp.stack(
        [(r ^ m) ^ (4 * a) for m in (0, 1, 3, 2) for a in range(2)] + [q, z, core, sign, x_hi]
    ).astype(jnp.int32)

    step = units // CHUNKS
    two_sems = [pltpu.SemaphoreType.DMA((2,))]
    near = row_flip(grad_out, 4)
    cross = both_flip(grad_out, 4, 2)
    far = col_flip(grad_out, 2)
    other = col_flip(hidden, 2)
    piece = lax.dynamic_slice_in_dim(down_weight, (1 - x_hi) * 2 * units, 2 * units, 0)
    one_sem = [pltpu.SemaphoreType.DMA]
    (mine,) = call(
        pack_kernel,
        "pack",
        [((2, 2, 128, 512), BF16)],
        [VMEM] * 3 + [HBM],
        (near, far, cross, grad_out),
        scratch=one_sem,
        mib=PACK,
    )
    piece, tokens = call(
        order_kernel,
        "order",
        [(piece.shape, BF16), ((2, 32, width), BF16)],
        [SMEM, ANY, VMEM, HBM],
        (where, piece, other, hidden),
        out_specs=[ANY, VMEM],
        scratch=one_sem,
        mib=PACK,
        aliases={1: 0},
    )
    got = [col_flip(piece, 2)]
    y1, y3 = row_flip(mine, 1), row_flip(mine, 3)
    y2 = row_flip(y1, 3)
    lefts, rights = [tokens], [tokens]
    for _ in range(3):
        left, right = z_swap(rights[-1], 0), z_swap(lefts[-1], 1)
        lefts.append(left)
        rights.append(right)
    for j in range(1, CHUNKS):
        (piece,) = call(
            functools.partial(next_kernel, j, CHUNKS),
            "next_rows",
            [((2 * step, 512), BF16)],
            [SMEM, ANY] + [VMEM] * 3,
            (where, down_weight, y1, lefts[1], rights[1]),
            scratch=two_sems,
        )
        got.append(col_flip(piece, 2))
    hiddens = lefts + rights[1:] + [z_swap(rights[-1], 0)]
    hiddens += [col_flip(h, 1) for h in hiddens]

    buffers = [pltpu.VMEM((step, 512), BF16), pltpu.SemaphoreType.DMA]
    flops = 2 * step * 1024 * 1024
    (rows,) = call(
        rows_kernel,
        "rows",
        [((8, 128, 1024), BF16)],
        [SMEM] + [VMEM] * 6,
        (where, mine, y1, y3, y2, lefts[TIED], rights[TIED]),
        flops=10**10,
    )

    def sums(j, *before):
        first, rest = call(
            functools.partial(mate_kernel, j, CHUNKS),
            "mate_sums",
            [((3, step, 128), F32), ((5, step, 128), F32)],
            [SMEM, ANY] + [VMEM] * 4,
            (where, down_weight, got[j], rows, lefts[3], rights[3]),
            scratch=buffers,
            flops=flops,
        )
        (own,) = call(
            functools.partial(own_kernel, j, CHUNKS),
            "own_sums",
            [((8, step, 128), F32)],
            [SMEM, ANY, VMEM, VMEM] + [VMEM] * len(before),
            (where, down_weight, got[j], rows, *before),
            scratch=buffers,
            flops=flops,
        )
        return own, col_flip(first, 1), col_flip(rest, 1)

    weight_grad, mark = call(
        weight_kernel,
        "weight_sum",
        [((width, 512), BF16), ((16, 128), BF16)],
        [SMEM] + [VMEM] * 17,
        (where, rows, *hiddens),
        out_specs=[ANY, VMEM],
        scratch=[
            pltpu.VMEM((1024, 512), BF16),
            pltpu.VMEM((width, 512), BF16),
            pltpu.SemaphoreType.DMA((len(TILES),)),
        ],
        mib=16,
        flops=2 * 1024 * width * 512,
    )

    def send(kernel, name, part, size, *args, kept=0):
        left, right, *others = call(
            functools.partial(kernel, part),
            name,
            [((size, 128), F32)] * (2 + kept),
            [VMEM] * len(args),
            args,
        )
        return [z_swap(left, 0), z_swap(right, 1), *others]

    quarters = []
    size = step // PARTS
    for j in range(CHUNKS):
        own, first, rest = sums(j)
        parts = range(PARTS)
        got1 = [send(send1_kernel, "send1", p, size // 2, own, first) for p in parts]
        got2 = [send(send2_kernel, "send2", p, size, own, first, *got1[p]) for p in parts]
        got3 = [send(send3_kernel, "send3", p, size, own, rest, *got2[p], kept=3) for p in parts]
        came = []
        for p in parts:
            left, right, near, far, base = got3[p]
            tie = (mark,) if p == PARTS - 1 else ()
            came += [base, *send(send4_kernel, "send4", p, size, near, far, left, right, *tie)]
        (total,) = call(
            last_kernel, "last", [((step, 128), F32)], [VMEM] * len(came), came
        )
        total = total.astype(BF16).T.reshape(2, 64, step)
        kept = lax.dynamic_index_in_dim(total, x_hi, 0, keepdims=False)
        came = col_flip(lax.dynamic_index_in_dim(total, 1 - x_hi, 0, keepdims=False), 2)
        pair = jnp.stack([jnp.where(x_hi == 0, kept, came), jnp.where(x_hi == 0, came, kept)])
        pair = pair.reshape(2, 2, 32, step)
        kept = lax.dynamic_index_in_dim(pair, core, 1, keepdims=False)
        came = col_flip(lax.dynamic_index_in_dim(pair, 1 - core, 1, keepdims=False), 1)
        one, two = jnp.where(core == 0, kept, came), jnp.where(core == 0, came, kept)
        quarters.append([one[0], two[0], one[1], two[1]])
    hidden_grad = jnp.concatenate([h[t] for t in range(4) for h in quarters], axis=1)
    return weight_grad, hidden_grad


def solution(mesh):
    in_specs = (P("col", "row"), P("row", "col"), P("row", "col"))
    out_specs = (P("row", "col"), P("col", "row"))
    return jax.shard_map(
        on_device, mesh=mesh, in_specs=in_specs, out_specs=out_specs, check_vma=False
    )
```

time: 341 us -> 135 us (0.40)
  waiting for transfers between devices: 306 us -> 63.1 us
  starting transfers between devices: 0.11 us -> 53.8 us
  matrix products: 17 us -> 0 us
  Pallas kernels: 0 us -> 12.9 us
  between operations: 13.8 us -> 0.92 us
  local copies, waits for them, and re-layouts: 0.01 us -> 3.6 us
    reduce_scatter x1 -> x0, waiting for transfers between devices: 168 us -> none  [input_part(): lax.psum_scatter(lax.dot_general(grad_full, down_weight, (((1,), (1,)), (...]
    all_gather x2 -> x0, waiting for transfers between devices: 137 us -> none  [the longest x1 95.1 us: weight_part(): lax.all_gather(hidden, 'col', axis=0, tiled=True)]
    ppermute x0 -> x43, waiting for transfers between devices: none -> 63.1 us  [the longest x23 33.4 us: z_swap(): lax.ppermute(value, 'col', [(c, mate(c // 4) * 4 + c % 4) for c in range(...]
    ppermute x0 -> x43, starting transfers between devices: none -> 53.8 us  [the longest x15 31.5 us: col_flip(): return lax.ppermute(value, 'col', [(c, c ^ bits) for c in range(COLS)])]
    dot_general x2 -> x0, matrix products: 17 us -> none  [the longest x1 8.66 us: weight_part(): lax.dot_general(lax.all_gather(hidden, 'col', axis=0, tiled=True), grad_f...]
    pallas_call x0 -> x15, Pallas kernels: none -> 12.9 us  [call(): pl.pallas_call(kernel, out_shape=[jax.ShapeDtypeStruct(shape, dtype) for...]
  transfers between devices with their start and end apart: 3 -> 43, of which waited for: 3 -> 19; matrix products, arithmetic and copies ran while one was open for 5% -> 1% of each run, Pallas kernels for 0% -> 8%
where the time goes in v1:
time: 135 us; the launch traced here: 134 us
  waiting for transfers between devices  63.1 us (47%)
  starting transfers between devices  53.8 us (40%)
  Pallas kernels  12.9 us (10%)
  local copies, waits for them, and re-layouts  3.6 us (3%)
    ppermute x23, waiting for transfers between devices, z_swap(): lax.ppermute(value, 'col', [(c, mate(c // 4) * 4 + c % 4) for c in range(...  33.4 us
    ppermute x15, starting transfers between devices, col_flip(): return lax.ppermute(value, 'col', [(c, c ^ bits) for c in range(COLS)])  31.5 us
    ppermute x23, starting transfers between devices, z_swap(): lax.ppermute(value, 'col', [(c, mate(c // 4) * 4 + c % 4) for c in range(...  19.4 us
    pallas_call x15, Pallas kernels, call(): pl.pallas_call(kernel, out_shape=[jax.ShapeDtypeStruct(shape, dtype) for...  12.9 us
    ppermute x15, waiting for transfers between devices, col_flip(): return lax.ppermute(value, 'col', [(c, c ^ bits) for c in range(COLS)])  12.6 us
    ppermute x4, waiting for transfers between devices, row_flip(): return lax.ppermute(value, 'row', [(r, r ^ bits) for r in range(ROWS)])  10.8 us
    ppermute x1, waiting for transfers between devices, both_flip(): return lax.ppermute(value, ('row', 'col'), pairs)  6.36 us
  transfers between devices with their start and end apart: 43, of which 19 were waited for; matrix products, arithmetic and copies ran while one was open for 1% of the time, Pallas kernels for 8%

profile of v1, /device:TPU:1, one launch (start us, length us, event | category | flops | bytes accessed | tf_op | source)
XLA Modules:
  0.0 134.4 jit_solution(11871846077470336607)
XLA Ops:
  0.6 3.7 %collective-permute-start.1 = (bf16[128,512]{1,0:T(8,128)(2,1)}, bf16[128,512]{1,0:T(8,128)(2,1)S(1)}, u32[]{:S(2)}, u32[]{:S(2)}) collective-permute-start(bf16[128,512]{1,0:T(8,128)(2,1)} %own.1), channel_id=1, source_target_pairs={{0,2},{1,3},{2,0},{3,1},{4,6},{5,7},{6,4},{7,5},{8,10},{9,11},{10,... | collective-permute-start | bytes 393224 | tf_op jit(solution)/shard_map/ppermute | solution.py:20
  5.2 2.4 %collective-permute-start.6 = (bf16[32,3328]{1,0:T(8,128)(2,1)}, bf16[32,3328]{1,0:T(8,128)(2,1)S(1)}, u32[]{:S(2)}, u32[]{:S(2)}) collective-permute-start(bf16[32,3328]{1,0:T(8,128)(2,1)} %hidden.1), channel_id=1, source_target_pairs={{0,2},{1,3},{2,0},{3,1},{4,6},{5,7},{6,4},{7,5},{8,10},{9,11},{10,... | collective-permute-start | bytes 638984 | tf_op jit(solution)/shard_map/ppermute | solution.py:20
  7.7 2.9 %collective-permute-done.near = bf16[128,512]{1,0:T(8,128)(2,1)S(1)} collective-permute-done((bf16[128,512]{1,0:T(8,128)(2,1)}, bf16[128,512]{1,0:T(8,128)(2,1)S(1)}, u32[]{:S(2)}, u32[]{:S(2)}) %collective-permute-start) | collective-permute-done | bytes 131104 | tf_op jit(solution)/shard_map/ppermute | solution.py:24
  10.5 6.4 %collective-permute-done.2.cross = bf16[128,512]{1,0:T(8,128)(2,1)S(1)} collective-permute-done((bf16[128,512]{1,0:T(8,128)(2,1)}, bf16[128,512]{1,0:T(8,128)(2,1)S(1)}, u32[]{:S(2)}, u32[]{:S(2)}) %collective-permute-start.2) | collective-permute-done | bytes 131104 | tf_op jit(solution)/shard_map/ppermute | solution.py:33
  16.9 0.9 copy-done.2
  18.1 1.6 %constant_dynamic-slice_fusion.piece = bf16[1664,512]{1,0:T(8,128)(2,1)S(1)} fusion(bf16[3328,512]{1,0:T(8,128)(2,1)} %down.3, s32[]{:T(128)S(6)} %select_n.68), kind=kLoop, calls=%fused_computation.18 | loop fusion | bytes 3407876 | tf_op jit(solution)/shard_map/dynamic_slice | solution.py:255
  19.7 0.8 order.1
  20.6 1.9 %collective-permute-start.7 = (bf16[2,32,3328]{2,1,0:T(8,128)(2,1)S(1)}, bf16[2,32,3328]{2,1,0:T(8,128)(2,1)S(1)}, u32[]{:S(2)}, u32[]{:S(2)}) collective-permute-start(bf16[2,32,3328]{2,1,0:T(8,128)(2,1)S(1)} %get-tuple-element.30.refs_0_), channel_id=1, source_target_pairs={{0,28},{1,29},{2,30},{3,31},{4,8},{5,9},{6,10},{7,11},{8,4},{9,5},... | collective-permute-start | bytes 1277960 | tf_op jit(solution)/shard_map/ppermute | solution.py:40
  22.5 3.7 %collective-permute-start.22 = (bf16[1664,512]{1,0:T(8,128)(2,1)S(1)}, bf16[1664,512]{1,0:T(8,128)(2,1)S(1)}, u32[]{:S(2)}, u32[]{:S(2)}) collective-permute-start(bf16[1664,512]{1,0:T(8,128)(2,1)S(1)} %get-tuple-element.32), channel_id=1, source_target_pairs={{0,2},{1,3},{2,0},{3,1},{4,6},{5,7},{6,4},{7,5},{8,10},{9,11},{10,... | collective-permute-start | bytes 5111816 | tf_op jit(solution)/shard_map/ppermute | solution.py:20
  26.2 1.9 %collective-permute-start.4 = (bf16[2,2,128,512]{3,2,1,0:T(8,128)(2,1)S(1)}, bf16[2,2,128,512]{3,2,1,0:T(8,128)(2,1)S(1)}, u32[]{:S(2)}, u32[]{:S(2)}) collective-permute-start(bf16[2,2,128,512]{3,2,1,0:T(8,128)(2,1)S(1)} %pack.1.p0), channel_id=1, source_target_pairs={{0,96},{32,64},{64,32},{96,0},{128,224},{160,192},{192,160},{224,1... | collective-permute-start | bytes 1572872 | tf_op jit(solution)/shard_map/ppermute | solution.py:24
  28.1 2.4 %collective-permute-done.3.p1 = bf16[2,2,128,512]{3,2,1,0:T(8,128)(2,1)S(1)} collective-permute-done((bf16[2,2,128,512]{3,2,1,0:T(8,128)(2,1)S(1)}, bf16[2,2,128,512]{3,2,1,0:T(8,128)(2,1)S(1)}, u32[]{:S(2)}, u32[]{:S(2)}) %collective-permute-start.3) | collective-permute-done | bytes 524320 | tf_op jit(solution)/shard_map/ppermute | solution.py:24
  30.6 10.8 %collective-permute-done.10.refs_1_.refs_5_ = bf16[2,32,3328]{2,1,0:T(8,128)(2,1)S(1)} collective-permute-done((bf16[2,32,3328]{2,1,0:T(8,128)(2,1)S(1)}, bf16[2,32,3328]{2,1,0:T(8,128)(2,1)S(1)}, u32[]{:S(2)}, u32[]{:S(2)}) %collective-permute-start.10) | collective-permute-done | bytes 426016 | tf_op jit(solution)/shard_map/ppermute | solution.py:40
  41.4 2.1 %collective-permute-start.12 = (bf16[2,32,3328]{2,1,0:T(8,128)(2,1)S(1)}, bf16[2,32,3328]{2,1,0:T(8,128)(2,1)S(1)}, u32[]{:S(2)}, u32[]{:S(2)}) collective-permute-start(bf16[2,32,3328]{2,1,0:T(8,128)(2,1)S(1)} %collective-permute-done.8.refs_0_.refs_2_), channel_id=1, source_target_pairs={{0,28},{1,29},{2,30},{3,31},{4,8},{5,9},{6,10},{7,11},{8,4},{9,5},... | collective-permute-start | bytes 1277960 | tf_op jit(solution)/shard_map/ppermute | solution.py:40
  43.5 5.5 %collective-permute-done.5.p3 = bf16[2,2,128,512]{3,2,1,0:T(8,128)(2,1)S(1)} collective-permute-done((bf16[2,2,128,512]{3,2,1,0:T(8,128)(2,1)S(1)}, bf16[2,2,128,512]{3,2,1,0:T(8,128)(2,1)S(1)}, u32[]{:S(2)}, u32[]{:S(2)}) %collective-permute-start.5) | collective-permute-done | bytes 524320 | tf_op jit(solution)/shard_map/ppermute | solution.py:24
  49.1 0.7 rows.1
  49.8 3.5 %collective-permute-done.11.refs_3_.refs_0_ = bf16[2,32,3328]{2,1,0:T(8,128)(2,1)S(1)} collective-permute-done((bf16[2,32,3328]{2,1,0:T(8,128)(2,1)S(1)}, bf16[2,32,3328]{2,1,0:T(8,128)(2,1)S(1)}, u32[]{:S(2)}, u32[]{:S(2)}) %collective-permute-start.11) | collective-permute-done | bytes 426016 | tf_op jit(solution)/shard_map/ppermute | solution.py:40
  53.3 6.7 %collective-permute-done.22.got = bf16[1664,512]{1,0:T(8,128)(2,1)S(1)} collective-permute-done((bf16[1664,512]{1,0:T(8,128)(2,1)S(1)}, bf16[1664,512]{1,0:T(8,128)(2,1)S(1)}, u32[]{:S(2)}, u32[]{:S(2)}) %collective-permute-start.22) | collective-permute-done | bytes 1703968 | tf_op jit(solution)/shard_map/ppermute | solution.py:20
  60.0 2.7 %mate_sums.1 = (f32[3,832,128]{2,1,0:T(8,128)S(1)}, f32[5,832,128]{2,1,0:T(8,128)S(1)}) custom-call(s32[13]{0:T(128)S(1)} %stack.64.where, bf16[3328,512]{1,0:T(8,128)(2,1)S(1)} %copy-done, bf16[1664,512]{1,0:T(8,128)(2,1)S(1)} %collective-permute-done.22.got, bf16[8,128,1024]{2,1,0:T(8,128)(2,1)S(1)} %rows.1, ...), custom_call_target="tpu_custom_call" | custom-call | flops 1744830464 | bytes 1048576 | tf_op jit(solution)/shard_map/mate_sums/pallas_call | solution.py:49
  62.7 4.5 %collective-permute-start.23 = (f32[5,832,128]{2,1,0:T(8,128)S(1)}, f32[5,832,128]{2,1,0:T(8,128)S(1)}, u32[]{:S(2)}, u32[]{:S(2)}) collective-permute-start(f32[5,832,128]{2,1,0:T(8,128)S(1)} %get-tuple-element.33), channel_id=1, source_target_pairs={{0,1},{1,0},{2,3},{3,2},{4,5},{5,4},{6,7},{7,6},{8,9},{9,8},{10,11... | collective-permute-start | bytes 6389768 | tf_op jit(solution)/shard_map/ppermute | solution.py:20
  67.4 2.7 %own_sums.1.own = f32[8,832,128]{2,1,0:T(8,128)S(1)} custom-call(s32[13]{0:T(128)S(1)} %stack.64.where, bf16[3328,512]{1,0:T(8,128)(2,1)S(1)} %copy-done, bf16[1664,512]{1,0:T(8,128)(2,1)S(1)} %collective-permute-done.22.got, bf16[8,128,1024]{2,1,0:T(8,128)(2,1)S(1)} %rows.1), custom_call_target="tpu_custom_call" | custom-call | flops 1744830464 | bytes 1048576 | tf_op jit(solution)/shard_map/own_sums/pallas_call | solution.py:49
  70.1 2.7 %collective-permute-done.24.first = f32[3,832,128]{2,1,0:T(8,128)S(1)} collective-permute-done((f32[3,832,128]{2,1,0:T(8,128)S(1)}, f32[3,832,128]{2,1,0:T(8,128)S(1)}, u32[]{:S(2)}, u32[]{:S(2)}) %collective-permute-start.24) | collective-permute-done | bytes 1277984 | tf_op jit(solution)/shard_map/ppermute | solution.py:20
  72.9 1.4 %collective-permute-start.34 = (f32[208,128]{1,0:T(8,128)S(1)}, f32[208,128]{1,0:T(8,128)S(1)}, u32[]{:S(2)}, u32[]{:S(2)}) collective-permute-start(f32[208,128]{1,0:T(8,128)S(1)} %get-tuple-element.47), channel_id=1, source_target_pairs={{0,28},{1,29},{2,30},{3,31},{4,8},{5,9},{6,10},{7,11},{8,4},{9,5},... | collective-permute-start | bytes 319496 | tf_op jit(solution)/shard_map/ppermute | solution.py:40
  74.4 0.8 collective-permute-start.25
  75.2 0.7 collective-permute-start.26
  75.9 1.2 collective-permute-done.33.came_left
  77.1 1.9 %collective-permute-start.14 = (bf16[2,32,3328]{2,1,0:T(8,128)(2,1)S(1)}, bf16[2,32,3328]{2,1,0:T(8,128)(2,1)S(1)}, u32[]{:S(2)}, u32[]{:S(2)}) collective-permute-start(bf16[2,32,3328]{2,1,0:T(8,128)(2,1)S(1)} %get-tuple-element.30.refs_0_), channel_id=1, source_target_pairs={{0,1},{1,0},{2,3},{3,2},{4,5},{5,4},{6,7},{7,6},{8,9},{9,8},{10,11... | collective-permute-start | bytes 1277960 | tf_op jit(solution)/shard_map/ppermute | solution.py:20
  79.6 0.9 collective-permute-start.18
  81.0 1.3 collective-permute-start.27
  82.3 1.4 %collective-permute-start.28 = (f32[416,128]{1,0:T(8,128)S(1)}, f32[416,128]{1,0:T(8,128)S(1)}, u32[]{:S(2)}, u32[]{:S(2)}) collective-permute-start(f32[416,128]{1,0:T(8,128)S(1)} %get-tuple-element.38), channel_id=1, source_target_pairs={{0,28},{1,29},{2,30},{3,31},{4,8},{5,9},{6,10},{7,11},{8,4},{9,5},... | collective-permute-start | bytes 638984 | tf_op jit(solution)/shard_map/ppermute | solution.py:40
  83.7 6.4 %collective-permute-done.13.refs_7_ = bf16[2,32,3328]{2,1,0:T(8,128)(2,1)S(1)} collective-permute-done((bf16[2,32,3328]{2,1,0:T(8,128)(2,1)S(1)}, bf16[2,32,3328]{2,1,0:T(8,128)(2,1)S(1)}, u32[]{:S(2)}, u32[]{:S(2)}) %collective-permute-start.13) | collective-permute-done | bytes 426016 | tf_op jit(solution)/shard_map/ppermute | solution.py:40
  90.1 2.0 %collective-permute-start.36 = (f32[416,128]{1,0:T(8,128)S(1)}, f32[416,128]{1,0:T(8,128)S(1)}, u32[]{:S(2)}, u32[]{:S(2)}) collective-permute-start(f32[416,128]{1,0:T(8,128)S(1)} %get-tuple-element.49), channel_id=1, source_target_pairs={{0,28},{1,29},{2,30},{3,31},{4,8},{5,9},{6,10},{7,11},{8,4},{9,5},... | collective-permute-start | bytes 638984 | tf_op jit(solution)/shard_map/ppermute | solution.py:40
  92.1 2.6 %collective-permute-done.27.came_left = f32[416,128]{1,0:T(8,128)S(1)} collective-permute-done((f32[416,128]{1,0:T(8,128)S(1)}, f32[416,128]{1,0:T(8,128)S(1)}, u32[]{:S(2)}, u32[]{:S(2)}) %collective-permute-start.27) | collective-permute-done | bytes 213024 | tf_op jit(solution)/shard_map/ppermute | solution.py:40
  94.7 5.0 %collective-permute-start.19 = (bf16[2,32,3328]{2,1,0:T(8,128)(2,1)S(1)}, bf16[2,32,3328]{2,1,0:T(8,128)(2,1)S(1)}, u32[]{:S(2)}, u32[]{:S(2)}) collective-permute-start(bf16[2,32,3328]{2,1,0:T(8,128)(2,1)S(1)} %collective-permute-done.10.refs_1_.refs_5_), channel_id=1, source_target_pairs={{0,1},{1,0},{2,3},{3,2},{4,5},{5,4},{6,7},{7,6},{8,9},{9,8},{10,11... | collective-permute-start | bytes 1277960 | tf_op jit(solution)/shard_map/ppermute | solution.py:20
  99.7 2.3 %collective-permute-start.17 = (bf16[2,32,3328]{2,1,0:T(8,128)(2,1)S(1)}, bf16[2,32,3328]{2,1,0:T(8,128)(2,1)S(1)}, u32[]{:S(2)}, u32[]{:S(2)}) collective-permute-start(bf16[2,32,3328]{2,1,0:T(8,128)(2,1)S(1)} %collective-permute-done.11.refs_3_.refs_0_), channel_id=1, source_target_pairs={{0,1},{1,0},{2,3},{3,2},{4,5},{5,4},{6,7},{7,6},{8,9},{9,8},{10,11... | collective-permute-start | bytes 1277960 | tf_op jit(solution)/shard_map/ppermute | solution.py:20
  103.1 1.5 %collective-permute-start.38 = (f32[416,128]{1,0:T(8,128)S(1)}, f32[416,128]{1,0:T(8,128)S(1)}, u32[]{:S(2)}, u32[]{:S(2)}) collective-permute-start(f32[416,128]{1,0:T(8,128)S(1)} %get-tuple-element.54), channel_id=1, source_target_pairs={{0,28},{1,29},{2,30},{3,31},{4,8},{5,9},{6,10},{7,11},{8,4},{9,5},... | collective-permute-start | bytes 638984 | tf_op jit(solution)/shard_map/ppermute | solution.py:40
  105.0 1.4 %collective-permute-start.30 = (f32[416,128]{1,0:T(8,128)S(1)}, f32[416,128]{1,0:T(8,128)S(1)}, u32[]{:S(2)}, u32[]{:S(2)}) collective-permute-start(f32[416,128]{1,0:T(8,128)S(1)} %get-tuple-element.43), channel_id=1, source_target_pairs={{0,28},{1,29},{2,30},{3,31},{4,8},{5,9},{6,10},{7,11},{8,4},{9,5},... | collective-permute-start | bytes 638984 | tf_op jit(solution)/shard_map/ppermute | solution.py:40
  106.5 5.2 %weight_sum.1 = (bf16[3328,512]{1,0:T(8,128)(2,1)}, bf16[16,128]{1,0:T(8,128)(2,1)S(1)}) custom-call(s32[13]{0:T(128)S(1)} %stack.64.where, bf16[8,128,1024]{2,1,0:T(8,128)(2,1)S(1)} %rows.1, bf16[2,32,3328]{2,1,0:T(8,128)(2,1)S(1)} %get-tuple-element.30.refs_0_, bf16[2,32,3328]{2,1,0:T(8,128)(2,1)S(1)} %collective-permute-done.9.refs_1_, ...), custom_call_target="tpu_custom_call" | custom-call | flops 3489660928 | bytes 1048576 | tf_op jit(solution)/shard_map/weight_sum/pallas_call | solution.py:49
  112.2 1.2 collective-permute-start.40
  114.0 1.4 %collective-permute-done.30.came_right = f32[416,128]{1,0:T(8,128)S(1)} collective-permute-done((f32[416,128]{1,0:T(8,128)S(1)}, f32[416,128]{1,0:T(8,128)S(1)}, u32[]{:S(2)}, u32[]{:S(2)}) %collective-permute-start.30) | collective-permute-done | bytes 213024 | tf_op jit(solution)/shard_map/ppermute | solution.py:40
  115.6 1.8 %collective-permute-start.32 = (f32[416,128]{1,0:T(8,128)S(1)}, f32[416,128]{1,0:T(8,128)S(1)}, u32[]{:S(2)}, u32[]{:S(2)}) collective-permute-start(f32[416,128]{1,0:T(8,128)S(1)} %get-tuple-element.45), channel_id=1, source_target_pairs={{0,28},{1,29},{2,30},{3,31},{4,8},{5,9},{6,10},{7,11},{8,4},{9,5},... | collective-permute-start | bytes 638984 | tf_op jit(solution)/shard_map/ppermute | solution.py:40
  117.6 1.5 %collective-permute-done.40.refs_5_ = f32[416,128]{1,0:T(8,128)S(1)} collective-permute-done((f32[416,128]{1,0:T(8,128)S(1)}, f32[416,128]{1,0:T(8,128)S(1)}, u32[]{:S(2)}, u32[]{:S(2)}) %collective-permute-start.40) | collective-permute-done | bytes 213024 | tf_op jit(solution)/shard_map/ppermute | solution.py:40
  119.1 3.8 %collective-permute-done.31.refs_1_ = f32[416,128]{1,0:T(8,128)S(1)} collective-permute-done((f32[416,128]{1,0:T(8,128)S(1)}, f32[416,128]{1,0:T(8,128)S(1)}, u32[]{:S(2)}, u32[]{:S(2)}) %collective-permute-start.31) | collective-permute-done | bytes 213024 | tf_op jit(solution)/shard_map/ppermute | solution.py:40
  122.9 1.3 collective-permute-done.32.refs_2_
  124.5 3.1 %collective-permute-start.41 = (bf16[64,832]{1,0:T(8,128)(2,1)S(1)}, bf16[64,832]{1,0:T(8,128)(2,1)S(1)}, u32[]{:S(2)}, u32[]{:S(2)}) collective-permute-start(bf16[64,832]{1,0:T(8,128)(2,1)S(1)} %dynamic-slice_bitcast_fusion), channel_id=1, source_target_pairs={{0,2},{1,3},{2,0},{3,1},{4,6},{5,7},{6,4},{7,5},{8,10},{9,11},{10,... | collective-permute-start | bytes 319496 | tf_op jit(solution)/shard_map/ppermute | solution.py:20
  127.6 2.2 %collective-permute-done.41 = bf16[64,832]{1,0:T(8,128)(2,1)S(1)} collective-permute-done((bf16[64,832]{1,0:T(8,128)(2,1)S(1)}, bf16[64,832]{1,0:T(8,128)(2,1)S(1)}, u32[]{:S(2)}, u32[]{:S(2)}) %collective-permute-start.41) | collective-permute-done | bytes 106528 | tf_op jit(solution)/shard_map/ppermute | solution.py:20
  129.8 2.7 %collective-permute-start.42 = (bf16[2,32,832]{2,1,0:T(8,128)(2,1)S(1)}, bf16[2,32,832]{2,1,0:T(8,128)(2,1)S(1)}, u32[]{:S(2)}, u32[]{:S(2)}) collective-permute-start(bf16[2,32,832]{2,1,0:T(8,128)(2,1)S(1)} %fusion.1), channel_id=1, source_target_pairs={{0,1},{1,0},{2,3},{3,2},{4,5},{5,4},{6,7},{7,6},{8,9},{9,8},{10,11... | collective-permute-start | bytes 319496 | tf_op jit(solution)/shard_map/ppermute | solution.py:20
  132.6 1.0 collective-permute-done.42
  133.6 0.8 concatenate.4
  (69 shorter events, 6.2 us)
Async XLA Ops:
  0.6 7.0 %collective-permute-start.1 = (bf16[128,512]{1,0:T(8,128)(2,1)}, bf16[128,512]{1,0:T(8,128)(2,1)S(1)}, u32[]{:S(2)}, u32[]{:S(2)}) collective-permute-start(bf16[128,512]{1,0:T(8,128)(2,1)} %own.1), channel_id=1, source_target_pairs={{0,2},{1,3},{2,0},{3,1},{4,6},{5,7},{6,4},{7,5},{8,10},{9,11},{10,... | collective-permute-start | bytes 393224 | tf_op jit(solution)/shard_map/ppermute | solution.py:20
  4.3 6.2 %collective-permute-start = (bf16[128,512]{1,0:T(8,128)(2,1)}, bf16[128,512]{1,0:T(8,128)(2,1)S(1)}, u32[]{:S(2)}, u32[]{:S(2)}) collective-permute-start(bf16[128,512]{1,0:T(8,128)(2,1)} %own.1), channel_id=1, source_target_pairs={{0,128},{32,160},{64,192},{96,224},{128,0},{160,32},{192,64},{224,... | collective-permute-start | bytes 393224 | tf_op jit(solution)/shard_map/ppermute | solution.py:24
  4.6 12.3 %collective-permute-start.2 = (bf16[128,512]{1,0:T(8,128)(2,1)}, bf16[128,512]{1,0:T(8,128)(2,1)S(1)}, u32[]{:S(2)}, u32[]{:S(2)}) collective-permute-start(bf16[128,512]{1,0:T(8,128)(2,1)} %own.1), channel_id=1, source_target_pairs={{0,130},{1,131},{2,128},{3,129},{4,134},{5,135},{6,132},{7,133},{8... | collective-permute-start | bytes 393224 | tf_op jit(solution)/shard_map/ppermute | solution.py:33
  5.2 14.5 %collective-permute-start.6 = (bf16[32,3328]{1,0:T(8,128)(2,1)}, bf16[32,3328]{1,0:T(8,128)(2,1)S(1)}, u32[]{:S(2)}, u32[]{:S(2)}) collective-permute-start(bf16[32,3328]{1,0:T(8,128)(2,1)} %hidden.1), channel_id=1, source_target_pairs={{0,2},{1,3},{2,0},{3,1},{4,6},{5,7},{6,4},{7,5},{8,10},{9,11},{10,... | collective-permute-start | bytes 638984 | tf_op jit(solution)/shard_map/ppermute | solution.py:20
  7.6 12.0 %copy-start.1 = (bf16[32,3328]{1,0:T(8,128)(2,1)S(1)}, bf16[32,3328]{1,0:T(8,128)(2,1)}, u32[]{:S(2)}) copy-start(bf16[32,3328]{1,0:T(8,128)(2,1)} %hidden.1) | copy-start | bytes 638980
  16.9 0.9 copy-start.2
  18.0 12.5 %collective-permute-start.3 = (bf16[2,2,128,512]{3,2,1,0:T(8,128)(2,1)S(1)}, bf16[2,2,128,512]{3,2,1,0:T(8,128)(2,1)S(1)}, u32[]{:S(2)}, u32[]{:S(2)}) collective-permute-start(bf16[2,2,128,512]{3,2,1,0:T(8,128)(2,1)S(1)} %pack.1.p0), channel_id=1, source_target_pairs={{0,32},{32,0},{64,96},{96,64},{128,160},{160,128},{192,224},{224,1... | collective-permute-start | bytes 1572872 | tf_op jit(solution)/shard_map/ppermute | solution.py:24
  20.5 9.9 %collective-permute-start.9 = (bf16[2,32,3328]{2,1,0:T(8,128)(2,1)S(1)}, bf16[2,32,3328]{2,1,0:T(8,128)(2,1)S(1)}, u32[]{:S(2)}, u32[]{:S(2)}) collective-permute-start(bf16[2,32,3328]{2,1,0:T(8,128)(2,1)S(1)} %get-tuple-element.30.refs_0_), channel_id=1, source_target_pairs={{0,4},{1,5},{2,6},{3,7},{4,0},{5,1},{6,2},{7,3},{8,12},{9,13},{10,... | collective-permute-start | bytes 1277960 | tf_op jit(solution)/shard_map/ppermute | solution.py:40
  20.6 9.9 %collective-permute-start.7 = (bf16[2,32,3328]{2,1,0:T(8,128)(2,1)S(1)}, bf16[2,32,3328]{2,1,0:T(8,128)(2,1)S(1)}, u32[]{:S(2)}, u32[]{:S(2)}) collective-permute-start(bf16[2,32,3328]{2,1,0:T(8,128)(2,1)S(1)} %get-tuple-element.30.refs_0_), channel_id=1, source_target_pairs={{0,28},{1,29},{2,30},{3,31},{4,8},{5,9},{6,10},{7,11},{8,4},{9,5},... | collective-permute-start | bytes 1277960 | tf_op jit(solution)/shard_map/ppermute | solution.py:40
  22.5 37.5 %copy-start = (bf16[3328,512]{1,0:T(8,128)(2,1)S(1)}, bf16[3328,512]{1,0:T(8,128)(2,1)}, u32[]{:S(2)}) copy-start(bf16[3328,512]{1,0:T(8,128)(2,1)} %down.3) | copy-start | bytes 10223620
  22.5 37.5 %collective-permute-start.22 = (bf16[1664,512]{1,0:T(8,128)(2,1)S(1)}, bf16[1664,512]{1,0:T(8,128)(2,1)S(1)}, u32[]{:S(2)}, u32[]{:S(2)}) collective-permute-start(bf16[1664,512]{1,0:T(8,128)(2,1)S(1)} %get-tuple-element.32), channel_id=1, source_target_pairs={{0,2},{1,3},{2,0},{3,1},{4,6},{5,7},{6,4},{7,5},{8,10},{9,11},{10,... | collective-permute-start | bytes 5111816 | tf_op jit(solution)/shard_map/ppermute | solution.py:20
  26.2 17.3 %collective-permute-start.4 = (bf16[2,2,128,512]{3,2,1,0:T(8,128)(2,1)S(1)}, bf16[2,2,128,512]{3,2,1,0:T(8,128)(2,1)S(1)}, u32[]{:S(2)}, u32[]{:S(2)}) collective-permute-start(bf16[2,2,128,512]{3,2,1,0:T(8,128)(2,1)S(1)} %pack.1.p0), channel_id=1, source_target_pairs={{0,96},{32,64},{64,32},{96,0},{128,224},{160,192},{192,160},{224,1... | collective-permute-start | bytes 1572872 | tf_op jit(solution)/shard_map/ppermute | solution.py:24
  30.5 18.6 %collective-permute-start.5 = (bf16[2,2,128,512]{3,2,1,0:T(8,128)(2,1)S(1)}, bf16[2,2,128,512]{3,2,1,0:T(8,128)(2,1)S(1)}, u32[]{:S(2)}, u32[]{:S(2)}) collective-permute-start(bf16[2,2,128,512]{3,2,1,0:T(8,128)(2,1)S(1)} %collective-permute-done.3.p1), channel_id=1, source_target_pairs={{0,96},{32,64},{64,32},{96,0},{128,224},{160,192},{192,160},{224,1... | collective-permute-start | bytes 1572872 | tf_op jit(solution)/shard_map/ppermute | solution.py:24
  30.5 10.9 %collective-permute-start.10 = (bf16[2,32,3328]{2,1,0:T(8,128)(2,1)S(1)}, bf16[2,32,3328]{2,1,0:T(8,128)(2,1)S(1)}, u32[]{:S(2)}, u32[]{:S(2)}) collective-permute-start(bf16[2,32,3328]{2,1,0:T(8,128)(2,1)S(1)} %collective-permute-done.9.refs_1_), channel_id=1, source_target_pairs={{0,28},{1,29},{2,30},{3,31},{4,8},{5,9},{6,10},{7,11},{8,4},{9,5},... | collective-permute-start | bytes 1277960 | tf_op jit(solution)/shard_map/ppermute | solution.py:40
  30.5 10.9 %collective-permute-start.8 = (bf16[2,32,3328]{2,1,0:T(8,128)(2,1)S(1)}, bf16[2,32,3328]{2,1,0:T(8,128)(2,1)S(1)}, u32[]{:S(2)}, u32[]{:S(2)}) collective-permute-start(bf16[2,32,3328]{2,1,0:T(8,128)(2,1)S(1)} %collective-permute-done.7.refs_4_), channel_id=1, source_target_pairs={{0,4},{1,5},{2,6},{3,7},{4,0},{5,1},{6,2},{7,3},{8,12},{9,13},{10,... | collective-permute-start | bytes 1277960 | tf_op jit(solution)/shard_map/ppermute | solution.py:40
  41.4 11.9 %collective-permute-start.11 = (bf16[2,32,3328]{2,1,0:T(8,128)(2,1)S(1)}, bf16[2,32,3328]{2,1,0:T(8,128)(2,1)S(1)}, u32[]{:S(2)}, u32[]{:S(2)}) collective-permute-start(bf16[2,32,3328]{2,1,0:T(8,128)(2,1)S(1)} %collective-permute-done.10.refs_1_.refs_5_), channel_id=1, source_target_pairs={{0,4},{1,5},{2,6},{3,7},{4,0},{5,1},{6,2},{7,3},{8,12},{9,13},{10,... | collective-permute-start | bytes 1277960 | tf_op jit(solution)/shard_map/ppermute | solution.py:40
  41.4 11.9 %collective-permute-start.12 = (bf16[2,32,3328]{2,1,0:T(8,128)(2,1)S(1)}, bf16[2,32,3328]{2,1,0:T(8,128)(2,1)S(1)}, u32[]{:S(2)}, u32[]{:S(2)}) collective-permute-start(bf16[2,32,3328]{2,1,0:T(8,128)(2,1)S(1)} %collective-permute-done.8.refs_0_.refs_2_), channel_id=1, source_target_pairs={{0,28},{1,29},{2,30},{3,31},{4,8},{5,9},{6,10},{7,11},{8,4},{9,5},... | collective-permute-start | bytes 1277960 | tf_op jit(solution)/shard_map/ppermute | solution.py:40
  62.7 39.5 %collective-permute-start.23 = (f32[5,832,128]{2,1,0:T(8,128)S(1)}, f32[5,832,128]{2,1,0:T(8,128)S(1)}, u32[]{:S(2)}, u32[]{:S(2)}) collective-permute-start(f32[5,832,128]{2,1,0:T(8,128)S(1)} %get-tuple-element.33), channel_id=1, source_target_pairs={{0,1},{1,0},{2,3},{3,2},{4,5},{5,4},{6,7},{7,6},{8,9},{9,8},{10,11... | collective-permute-start | bytes 6389768 | tf_op jit(solution)/shard_map/ppermute | solution.py:20
  67.1 5.7 %collective-permute-start.24 = (f32[3,832,128]{2,1,0:T(8,128)S(1)}, f32[3,832,128]{2,1,0:T(8,128)S(1)}, u32[]{:S(2)}, u32[]{:S(2)}) collective-permute-start(f32[3,832,128]{2,1,0:T(8,128)S(1)} %get-tuple-element.34), channel_id=1, source_target_pairs={{0,1},{1,0},{2,3},{3,2},{4,5},{5,4},{6,7},{7,6},{8,9},{9,8},{10,11... | collective-permute-start | bytes 3833864 | tf_op jit(solution)/shard_map/ppermute | solution.py:20
  72.8 4.3 %collective-permute-start.33 = (f32[208,128]{1,0:T(8,128)S(1)}, f32[208,128]{1,0:T(8,128)S(1)}, u32[]{:S(2)}, u32[]{:S(2)}) collective-permute-start(f32[208,128]{1,0:T(8,128)S(1)} %get-tuple-element.46), channel_id=1, source_target_pairs={{0,4},{1,5},{2,6},{3,7},{4,0},{5,1},{6,2},{7,3},{8,12},{9,13},{10,... | collective-permute-start | bytes 319496 | tf_op jit(solution)/shard_map/ppermute | solution.py:40
  72.9 6.1 %collective-permute-start.34 = (f32[208,128]{1,0:T(8,128)S(1)}, f32[208,128]{1,0:T(8,128)S(1)}, u32[]{:S(2)}, u32[]{:S(2)}) collective-permute-start(f32[208,128]{1,0:T(8,128)S(1)} %get-tuple-element.47), channel_id=1, source_target_pairs={{0,28},{1,29},{2,30},{3,31},{4,8},{5,9},{6,10},{7,11},{8,4},{9,5},... | collective-permute-start | bytes 319496 | tf_op jit(solution)/shard_map/ppermute | solution.py:40
  74.4 5.2 %collective-permute-start.25 = (f32[208,128]{1,0:T(8,128)S(1)}, f32[208,128]{1,0:T(8,128)S(1)}, u32[]{:S(2)}, u32[]{:S(2)}) collective-permute-start(f32[208,128]{1,0:T(8,128)S(1)} %get-tuple-element.35), channel_id=1, source_target_pairs={{0,4},{1,5},{2,6},{3,7},{4,0},{5,1},{6,2},{7,3},{8,12},{9,13},{10,... | collective-permute-start | bytes 319496 | tf_op jit(solution)/shard_map/ppermute | solution.py:40
  75.2 5.4 %collective-permute-start.26 = (f32[208,128]{1,0:T(8,128)S(1)}, f32[208,128]{1,0:T(8,128)S(1)}, u32[]{:S(2)}, u32[]{:S(2)}) collective-permute-start(f32[208,128]{1,0:T(8,128)S(1)} %get-tuple-element.36), channel_id=1, source_target_pairs={{0,28},{1,29},{2,30},{3,31},{4,8},{5,9},{6,10},{7,11},{8,4},{9,5},... | collective-permute-start | bytes 319496 | tf_op jit(solution)/shard_map/ppermute | solution.py:40
  77.1 3.9 %collective-permute-start.14 = (bf16[2,32,3328]{2,1,0:T(8,128)(2,1)S(1)}, bf16[2,32,3328]{2,1,0:T(8,128)(2,1)S(1)}, u32[]{:S(2)}, u32[]{:S(2)}) collective-permute-start(bf16[2,32,3328]{2,1,0:T(8,128)(2,1)S(1)} %get-tuple-element.30.refs_0_), channel_id=1, source_target_pairs={{0,1},{1,0},{2,3},{3,2},{4,5},{5,4},{6,7},{7,6},{8,9},{9,8},{10,11... | collective-permute-start | bytes 1277960 | tf_op jit(solution)/shard_map/ppermute | solution.py:20
  79.0 3.2 %collective-permute-start.15 = (bf16[2,32,3328]{2,1,0:T(8,128)(2,1)S(1)}, bf16[2,32,3328]{2,1,0:T(8,128)(2,1)S(1)}, u32[]{:S(2)}, u32[]{:S(2)}) collective-permute-start(bf16[2,32,3328]{2,1,0:T(8,128)(2,1)S(1)} %collective-permute-done.9.refs_1_), channel_id=1, source_target_pairs={{0,1},{1,0},{2,3},{3,2},{4,5},{5,4},{6,7},{7,6},{8,9},{9,8},{10,11... | collective-permute-start | bytes 1277960 | tf_op jit(solution)/shard_map/ppermute | solution.py:20
  79.6 4.1 %collective-permute-start.18 = (bf16[2,32,3328]{2,1,0:T(8,128)(2,1)S(1)}, bf16[2,32,3328]{2,1,0:T(8,128)(2,1)S(1)}, u32[]{:S(2)}, u32[]{:S(2)}) collective-permute-start(bf16[2,32,3328]{2,1,0:T(8,128)(2,1)S(1)} %collective-permute-done.7.refs_4_), channel_id=1, source_target_pairs={{0,1},{1,0},{2,3},{3,2},{4,5},{5,4},{6,7},{7,6},{8,9},{9,8},{10,11... | collective-permute-start | bytes 1277960 | tf_op jit(solution)/shard_map/ppermute | solution.py:20
  80.6 9.5 %collective-permute-start.13 = (bf16[2,32,3328]{2,1,0:T(8,128)(2,1)S(1)}, bf16[2,32,3328]{2,1,0:T(8,128)(2,1)S(1)}, u32[]{:S(2)}, u32[]{:S(2)}) collective-permute-start(bf16[2,32,3328]{2,1,0:T(8,128)(2,1)S(1)} %collective-permute-done.12.refs_6_.refs_1_), channel_id=1, source_target_pairs={{0,4},{1,5},{2,6},{3,7},{4,0},{5,1},{6,2},{7,3},{8,12},{9,13},{10,... | collective-permute-start | bytes 1277960 | tf_op jit(solution)/shard_map/ppermute | solution.py:40
  81.0 13.7 %collective-permute-start.27 = (f32[416,128]{1,0:T(8,128)S(1)}, f32[416,128]{1,0:T(8,128)S(1)}, u32[]{:S(2)}, u32[]{:S(2)}) collective-permute-start(f32[416,128]{1,0:T(8,128)S(1)} %get-tuple-element.37), channel_id=1, source_target_pairs={{0,4},{1,5},{2,6},{3,7},{4,0},{5,1},{6,2},{7,3},{8,12},{9,13},{10,... | collective-permute-start | bytes 638984 | tf_op jit(solution)/shard_map/ppermute | solution.py:40
  82.3 17.4 %collective-permute-start.28 = (f32[416,128]{1,0:T(8,128)S(1)}, f32[416,128]{1,0:T(8,128)S(1)}, u32[]{:S(2)}, u32[]{:S(2)}) collective-permute-start(f32[416,128]{1,0:T(8,128)S(1)} %get-tuple-element.38), channel_id=1, source_target_pairs={{0,28},{1,29},{2,30},{3,31},{4,8},{5,9},{6,10},{7,11},{8,4},{9,5},... | collective-permute-start | bytes 638984 | tf_op jit(solution)/shard_map/ppermute | solution.py:40
  83.7 15.9 %collective-permute-start.35 = (f32[416,128]{1,0:T(8,128)S(1)}, f32[416,128]{1,0:T(8,128)S(1)}, u32[]{:S(2)}, u32[]{:S(2)}) collective-permute-start(f32[416,128]{1,0:T(8,128)S(1)} %get-tuple-element.48), channel_id=1, source_target_pairs={{0,4},{1,5},{2,6},{3,7},{4,0},{5,1},{6,2},{7,3},{8,12},{9,13},{10,... | collective-permute-start | bytes 638984 | tf_op jit(solution)/shard_map/ppermute | solution.py:40
  90.1 11.8 %collective-permute-start.36 = (f32[416,128]{1,0:T(8,128)S(1)}, f32[416,128]{1,0:T(8,128)S(1)}, u32[]{:S(2)}, u32[]{:S(2)}) collective-permute-start(f32[416,128]{1,0:T(8,128)S(1)} %get-tuple-element.49), channel_id=1, source_target_pairs={{0,28},{1,29},{2,30},{3,31},{4,8},{5,9},{6,10},{7,11},{8,4},{9,5},... | collective-permute-start | bytes 638984 | tf_op jit(solution)/shard_map/ppermute | solution.py:40
  94.7 8.0 %collective-permute-start.19 = (bf16[2,32,3328]{2,1,0:T(8,128)(2,1)S(1)}, bf16[2,32,3328]{2,1,0:T(8,128)(2,1)S(1)}, u32[]{:S(2)}, u32[]{:S(2)}) collective-permute-start(bf16[2,32,3328]{2,1,0:T(8,128)(2,1)S(1)} %collective-permute-done.10.refs_1_.refs_5_), channel_id=1, source_target_pairs={{0,1},{1,0},{2,3},{3,2},{4,5},{5,4},{6,7},{7,6},{8,9},{9,8},{10,11... | collective-permute-start | bytes 1277960 | tf_op jit(solution)/shard_map/ppermute | solution.py:20
  99.7 3.5 %collective-permute-start.16 = (bf16[2,32,3328]{2,1,0:T(8,128)(2,1)S(1)}, bf16[2,32,3328]{2,1,0:T(8,128)(2,1)S(1)}, u32[]{:S(2)}, u32[]{:S(2)}) collective-permute-start(bf16[2,32,3328]{2,1,0:T(8,128)(2,1)S(1)} %collective-permute-done.8.refs_0_.refs_2_), channel_id=1, source_target_pairs={{0,1},{1,0},{2,3},{3,2},{4,5},{5,4},{6,7},{7,6},{8,9},{9,8},{10,11... | collective-permute-start | bytes 1277960 | tf_op jit(solution)/shard_map/ppermute | solution.py:20
  99.7 4.9 %collective-permute-start.17 = (bf16[2,32,3328]{2,1,0:T(8,128)(2,1)S(1)}, bf16[2,32,3328]{2,1,0:T(8,128)(2,1)S(1)}, u32[]{:S(2)}, u32[]{:S(2)}) collective-permute-start(bf16[2,32,3328]{2,1,0:T(8,128)(2,1)S(1)} %collective-permute-done.11.refs_3_.refs_0_), channel_id=1, source_target_pairs={{0,1},{1,0},{2,3},{3,2},{4,5},{5,4},{6,7},{7,6},{8,9},{9,8},{10,11... | collective-permute-start | bytes 1277960 | tf_op jit(solution)/shard_map/ppermute | solution.py:20
  101.9 3.1 %collective-permute-start.20 = (bf16[2,32,3328]{2,1,0:T(8,128)(2,1)S(1)}, bf16[2,32,3328]{2,1,0:T(8,128)(2,1)S(1)}, u32[]{:S(2)}, u32[]{:S(2)}) collective-permute-start(bf16[2,32,3328]{2,1,0:T(8,128)(2,1)S(1)} %collective-permute-done.12.refs_6_.refs_1_), channel_id=1, source_target_pairs={{0,1},{1,0},{2,3},{3,2},{4,5},{5,4},{6,7},{7,6},{8,9},{9,8},{10,11... | collective-permute-start | bytes 1277960 | tf_op jit(solution)/shard_map/ppermute | solution.py:20
  102.2 4.3 %collective-permute-start.21 = (bf16[2,32,3328]{2,1,0:T(8,128)(2,1)S(1)}, bf16[2,32,3328]{2,1,0:T(8,128)(2,1)S(1)}, u32[]{:S(2)}, u32[]{:S(2)}) collective-permute-start(bf16[2,32,3328]{2,1,0:T(8,128)(2,1)S(1)} %collective-permute-done.13.refs_7_), channel_id=1, source_target_pairs={{0,1},{1,0},{2,3},{3,2},{4,5},{5,4},{6,7},{7,6},{8,9},{9,8},{10,11... | collective-permute-start | bytes 1277960 | tf_op jit(solution)/shard_map/ppermute | solution.py:20
  102.7 9.0 %collective-permute-start.37 = (f32[416,128]{1,0:T(8,128)S(1)}, f32[416,128]{1,0:T(8,128)S(1)}, u32[]{:S(2)}, u32[]{:S(2)}) collective-permute-start(f32[416,128]{1,0:T(8,128)S(1)} %get-tuple-element.53), channel_id=1, source_target_pairs={{0,4},{1,5},{2,6},{3,7},{4,0},{5,1},{6,2},{7,3},{8,12},{9,13},{10,... | collective-permute-start | bytes 638984 | tf_op jit(solution)/shard_map/ppermute | solution.py:40
  103.1 8.6 %collective-permute-start.38 = (f32[416,128]{1,0:T(8,128)S(1)}, f32[416,128]{1,0:T(8,128)S(1)}, u32[]{:S(2)}, u32[]{:S(2)}) collective-permute-start(f32[416,128]{1,0:T(8,128)S(1)} %get-tuple-element.54), channel_id=1, source_target_pairs={{0,28},{1,29},{2,30},{3,31},{4,8},{5,9},{6,10},{7,11},{8,4},{9,5},... | collective-permute-start | bytes 638984 | tf_op jit(solution)/shard_map/ppermute | solution.py:40
  104.6 9.4 %collective-permute-start.29 = (f32[416,128]{1,0:T(8,128)S(1)}, f32[416,128]{1,0:T(8,128)S(1)}, u32[]{:S(2)}, u32[]{:S(2)}) collective-permute-start(f32[416,128]{1,0:T(8,128)S(1)} %get-tuple-element.42), channel_id=1, source_target_pairs={{0,4},{1,5},{2,6},{3,7},{4,0},{5,1},{6,2},{7,3},{8,12},{9,13},{10,... | collective-permute-start | bytes 638984 | tf_op jit(solution)/shard_map/ppermute | solution.py:40
  105.0 10.4 %collective-permute-start.30 = (f32[416,128]{1,0:T(8,128)S(1)}, f32[416,128]{1,0:T(8,128)S(1)}, u32[]{:S(2)}, u32[]{:S(2)}) collective-permute-start(f32[416,128]{1,0:T(8,128)S(1)} %get-tuple-element.43), channel_id=1, source_target_pairs={{0,28},{1,29},{2,30},{3,31},{4,8},{5,9},{6,10},{7,11},{8,4},{9,5},... | collective-permute-start | bytes 638984 | tf_op jit(solution)/shard_map/ppermute | solution.py:40
  111.8 5.8 %collective-permute-start.39 = (f32[416,128]{1,0:T(8,128)S(1)}, f32[416,128]{1,0:T(8,128)S(1)}, u32[]{:S(2)}, u32[]{:S(2)}) collective-permute-start(f32[416,128]{1,0:T(8,128)S(1)} %get-tuple-element.56), channel_id=1, source_target_pairs={{0,4},{1,5},{2,6},{3,7},{4,0},{5,1},{6,2},{7,3},{8,12},{9,13},{10,... | collective-permute-start | bytes 638984 | tf_op jit(solution)/shard_map/ppermute | solution.py:40
  112.2 6.9 %collective-permute-start.40 = (f32[416,128]{1,0:T(8,128)S(1)}, f32[416,128]{1,0:T(8,128)S(1)}, u32[]{:S(2)}, u32[]{:S(2)}) collective-permute-start(f32[416,128]{1,0:T(8,128)S(1)} %get-tuple-element.57), channel_id=1, source_target_pairs={{0,28},{1,29},{2,30},{3,31},{4,8},{5,9},{6,10},{7,11},{8,4},{9,5},... | collective-permute-start | bytes 638984 | tf_op jit(solution)/shard_map/ppermute | solution.py:40
  115.5 7.4 %collective-permute-start.31 = (f32[416,128]{1,0:T(8,128)S(1)}, f32[416,128]{1,0:T(8,128)S(1)}, u32[]{:S(2)}, u32[]{:S(2)}) collective-permute-start(f32[416,128]{1,0:T(8,128)S(1)} %get-tuple-element.44), channel_id=1, source_target_pairs={{0,4},{1,5},{2,6},{3,7},{4,0},{5,1},{6,2},{7,3},{8,12},{9,13},{10,... | collective-permute-start | bytes 638984 | tf_op jit(solution)/shard_map/ppermute | solution.py:40
  115.6 8.6 %collective-permute-start.32 = (f32[416,128]{1,0:T(8,128)S(1)}, f32[416,128]{1,0:T(8,128)S(1)}, u32[]{:S(2)}, u32[]{:S(2)}) collective-permute-start(f32[416,128]{1,0:T(8,128)S(1)} %get-tuple-element.45), channel_id=1, source_target_pairs={{0,28},{1,29},{2,30},{3,31},{4,8},{5,9},{6,10},{7,11},{8,4},{9,5},... | collective-permute-start | bytes 638984 | tf_op jit(solution)/shard_map/ppermute | solution.py:40
  124.5 5.2 %collective-permute-start.41 = (bf16[64,832]{1,0:T(8,128)(2,1)S(1)}, bf16[64,832]{1,0:T(8,128)(2,1)S(1)}, u32[]{:S(2)}, u32[]{:S(2)}) collective-permute-start(bf16[64,832]{1,0:T(8,128)(2,1)S(1)} %dynamic-slice_bitcast_fusion), channel_id=1, source_target_pairs={{0,2},{1,3},{2,0},{3,1},{4,6},{5,7},{6,4},{7,5},{8,10},{9,11},{10,... | collective-permute-start | bytes 319496 | tf_op jit(solution)/shard_map/ppermute | solution.py:20
  129.8 3.7 %collective-permute-start.42 = (bf16[2,32,832]{2,1,0:T(8,128)(2,1)S(1)}, bf16[2,32,832]{2,1,0:T(8,128)(2,1)S(1)}, u32[]{:S(2)}, u32[]{:S(2)}) collective-permute-start(bf16[2,32,832]{2,1,0:T(8,128)(2,1)S(1)} %fusion.1), channel_id=1, source_target_pairs={{0,1},{1,0},{2,3},{3,2},{4,5},{5,4},{6,7},{7,6},{8,9},{9,8},{10,11... | collective-permute-start | bytes 319496 | tf_op jit(solution)/shard_map/ppermute | solution.py:20

commit v2 on v1

--- a/solution.py
+++ b/solution.py
@@ -8,6 +8,7 @@
 from jax.sharding import PartitionSpec as P
 
 ROWS, COLS, Z = 8, 32, 8
+THIRD, FOURTH = None, None
 CHUNKS, PARTS, TIED, MARK, PACK = 1, 2, 2, 3, 40
 F32, BF16 = jnp.float32, jnp.bfloat16
 ANY = pl.BlockSpec(memory_space=pl.ANY)
@@ -77,21 +78,20 @@
     return copies
 
 
-def pack_kernel(near, far, cross, own, out, sem):
-    copy = pltpu.make_async_copy(own, out.at[0, 0], sem)
-    copy.start()
+def pack_kernel(where, piece, near, far, cross, other, own, hidden, same, out, tokens, sems):
+    x_hi = where[X_HI]
+    copies = [
+        pltpu.make_async_copy(own, out.at[0, 0], sems.at[0]),
+        pltpu.make_async_copy(hidden, tokens.at[x_hi], sems.at[1]),
+    ]
+    for copy in copies:
+        copy.start()
     out[0, 1] = far[...]
     out[1, 0] = near[...]
     out[1, 1] = cross[...]
-    copy.wait()
-
-
-def order_kernel(where, piece, other, hidden, same, tokens, sem):
-    x_hi = where[X_HI]
-    copy = pltpu.make_async_copy(hidden, tokens.at[x_hi], sem)
-    copy.start()
     tokens[1 - x_hi] = other[...]
-    copy.wait()
+    for copy in copies:
+        copy.wait()
 
 
 def next_kernel(chunk, chunks, where, down, *refs):
@@ -164,14 +164,16 @@
     return slice(part * size, part * size + size)
 
 
-def send1_kernel(part, own, first, left, right):
+def send1_kernel(part, own, first, *refs):
+    left, right = refs[-2:]
     half = left.shape[0]
     lower, upper = part_of(2 * part, half), part_of(2 * part + 1, half)
     left[...] = own[4, lower] + first[0, lower]
     right[...] = own[4, upper] + first[0, upper]
 
 
-def send2_kernel(part, own, first, came_left, came_right, left, right):
+def send2_kernel(part, own, first, came_left, came_right, *refs):
+    left, right = refs[-2:]
     half = came_left.shape[0]
     lower, upper = part_of(2 * part, half), part_of(2 * part + 1, half)
     left[:half] = own[3, lower] + first[1, lower]
@@ -180,7 +182,8 @@
     right[half:] = own[5, upper] + first[2, upper]
 
 
-def send3_kernel(part, own, rest, came_left, came_right, left, right, near, far, base):
+def send3_kernel(part, own, rest, came_left, came_right, *refs):
+    left, right, near, far, base = refs[-5:]
     at = part_of(part, left.shape[0])
     left[...] = own[2, at] + rest[0, at] + came_right[...]
     right[...] = own[6, at] + rest[1, at] + came_left[...]
@@ -253,24 +256,14 @@
     far = col_flip(grad_out, 2)
     other = col_flip(hidden, 2)
     piece = lax.dynamic_slice_in_dim(down_weight, (1 - x_hi) * 2 * units, 2 * units, 0)
-    one_sem = [pltpu.SemaphoreType.DMA]
-    (mine,) = call(
+    piece, mine, tokens = call(
         pack_kernel,
         "pack",
-        [((2, 2, 128, 512), BF16)],
-        [VMEM] * 3 + [HBM],
-        (near, far, cross, grad_out),
-        scratch=one_sem,
-        mib=PACK,
-    )
-    piece, tokens = call(
-        order_kernel,
-        "order",
-        [(piece.shape, BF16), ((2, 32, width), BF16)],
-        [SMEM, ANY, VMEM, HBM],
-        (where, piece, other, hidden),
-        out_specs=[ANY, VMEM],
-        scratch=one_sem,
+        [(piece.shape, BF16), ((2, 2, 128, 512), BF16), ((2, 32, width), BF16)],
+        [SMEM, ANY] + [VMEM] * 4 + [HBM] * 2,
+        (where, piece, near, far, cross, other, grad_out, hidden),
+        out_specs=[ANY, VMEM, VMEM],
+        scratch=two_sems,
         mib=PACK,
         aliases={1: 0},
     )
@@ -303,7 +296,7 @@
         [((8, 128, 1024), BF16)],
         [SMEM] + [VMEM] * 6,
         (where, mine, y1, y3, y2, lefts[TIED], rights[TIED]),
-        flops=10**10,
+        flops=5 * 10**9,
     )
 
     def sums(j, *before):
@@ -353,14 +346,18 @@
         )
         return [z_swap(left, 0), z_swap(right, 1), *others]
 
+    def ties(stage, part):
+        third = (lefts[3], rights[3]) if (stage, part) == THIRD else ()
+        return third + ((hiddens[7],) if (stage, part) == FOURTH else ())
+
     quarters = []
     size = step // PARTS
     for j in range(CHUNKS):
-        own, first, rest = sums(j)
+        own, first, rest = sums(j, *ties(0, 0))
         parts = range(PARTS)
-        got1 = [send(send1_kernel, "send1", p, size // 2, own, first) for p in parts]
-        got2 = [send(send2_kernel, "send2", p, size, own, first, *got1[p]) for p in parts]
-        got3 = [send(send3_kernel, "send3", p, size, own, rest, *got2[p], kept=3) for p in parts]
+        got1 = [send(send1_kernel, "send1", p, size // 2, own, first, *ties(1, p)) for p in parts]
+        got2 = [send(send2_kernel, "send2", p, size, own, first, *got1[p], *ties(2, p)) for p in parts]
+        got3 = [send(send3_kernel, "send3", p, size, own, rest, *got2[p], *ties(3, p), kept=3) for p in parts]
         came = []
         for p in parts:
             left, right, near, far, base = got3[p]

time: 135 us -> 133 us (0.985)
  waiting for transfers between devices: 63.1 us -> 52.8 us
  starting transfers between devices: 53.8 us -> 63 us
    ppermute x23, starting transfers between devices: 19.4 us -> 27.6 us  [z_swap(): lax.ppermute(value, 'col', [(c, mate(c // 4) * 4 + c % 4) for c in range(...]
    ppermute x15, waiting for transfers between devices: 12.6 us -> 6.51 us  [col_flip(): return lax.ppermute(value, 'col', [(c, c ^ bits) for c in range(COLS)])]
    ppermute x4, waiting for transfers between devices: 10.8 us -> 4.74 us  [row_flip(): return lax.ppermute(value, 'row', [(r, r ^ bits) for r in range(ROWS)])]
    ppermute x4, starting transfers between devices: 2.31 us -> 6.24 us  [row_flip(): return lax.ppermute(value, 'row', [(r, r ^ bits) for r in range(ROWS)])]
    ppermute x15, starting transfers between devices: 31.5 us -> 28.6 us  [col_flip(): return lax.ppermute(value, 'col', [(c, c ^ bits) for c in range(COLS)])]
    ppermute x23, waiting for transfers between devices: 33.4 us -> 35.2 us  [z_swap(): lax.ppermute(value, 'col', [(c, mate(c // 4) * 4 + c % 4) for c in range(...]
    pallas_call x15 -> x14, Pallas kernels: 12.9 us -> 12.9 us  [call(): pl.pallas_call(kernel, out_shape=[jax.ShapeDtypeStruct(shape, dtype) for...]
  transfers between devices with their start and end apart: 43 -> 43, of which waited for: 19 -> 19; matrix products, arithmetic and copies ran while one was open for 1% -> 1% of each run, Pallas kernels for 8% -> 7%
where the time goes in v2:
time: 133 us; the launch traced here: 132 us
  starting transfers between devices  63 us (47%)
  waiting for transfers between devices  52.8 us (40%)
  Pallas kernels  12.9 us (10%)
  local copies, waits for them, and re-layouts  2.69 us (2%)
    ppermute x23, waiting for transfers between devices, z_swap(): lax.ppermute(value, 'col', [(c, mate(c // 4) * 4 + c % 4) for c in range(...  35.2 us
    ppermute x15, starting transfers between devices, col_flip(): return lax.ppermute(value, 'col', [(c, c ^ bits) for c in range(COLS)])  28.6 us
    ppermute x23, starting transfers between devices, z_swap(): lax.ppermute(value, 'col', [(c, mate(c // 4) * 4 + c % 4) for c in range(...  27.6 us
    pallas_call x14, Pallas kernels, call(): pl.pallas_call(kernel, out_shape=[jax.ShapeDtypeStruct(shape, dtype) for...  12.9 us
    ppermute x15, waiting for transfers between devices, col_flip(): return lax.ppermute(value, 'col', [(c, c ^ bits) for c in range(COLS)])  6.51 us
    ppermute x1, waiting for transfers between devices, both_flip(): return lax.ppermute(value, ('row', 'col'), pairs)  6.36 us
    ppermute x4, starting transfers between devices, row_flip(): return lax.ppermute(value, 'row', [(r, r ^ bits) for r in range(ROWS)])  6.24 us
    ppermute x4, waiting for transfers between devices, row_flip(): return lax.ppermute(value, 'row', [(r, r ^ bits) for r in range(ROWS)])  4.74 us
  transfers between devices with their start and end apart: 43, of which 19 were waited for; matrix products, arithmetic and copies ran while one was open for 1% of the time, Pallas kernels for 7%

profile of v2, /device:TPU:1, one launch (start us, length us, event | category | flops | bytes accessed | tf_op | source)
XLA Modules:
  0.0 132.5 jit_solution(8279683343569324447)
XLA Ops:
  0.6 3.7 %collective-permute-start.1 = (bf16[128,512]{1,0:T(8,128)(2,1)}, bf16[128,512]{1,0:T(8,128)(2,1)S(1)}, u32[]{:S(2)}, u32[]{:S(2)}) collective-permute-start(bf16[128,512]{1,0:T(8,128)(2,1)} %own.1), channel_id=1, source_target_pairs={{0,2},{1,3},{2,0},{3,1},{4,6},{5,7},{6,4},{7,5},{8,10},{9,11},{10,... | collective-permute-start | bytes 393224 | tf_op jit(solution)/shard_map/ppermute | solution.py:21
  5.2 2.4 %collective-permute-start.3 = (bf16[32,3328]{1,0:T(8,128)(2,1)}, bf16[32,3328]{1,0:T(8,128)(2,1)S(1)}, u32[]{:S(2)}, u32[]{:S(2)}) collective-permute-start(bf16[32,3328]{1,0:T(8,128)(2,1)} %hidden.1), channel_id=1, source_target_pairs={{0,2},{1,3},{2,0},{3,1},{4,6},{5,7},{6,4},{7,5},{8,10},{9,11},{10,... | collective-permute-start | bytes 638984 | tf_op jit(solution)/shard_map/ppermute | solution.py:21
  7.6 1.6 %constant_dynamic-slice_fusion.piece = bf16[1664,512]{1,0:T(8,128)(2,1)S(1)} fusion(bf16[3328,512]{1,0:T(8,128)(2,1)} %down.3, s32[]{:T(128)S(6)} %select_n.68), kind=kLoop, calls=%fused_computation.18 | loop fusion | bytes 3407876 | tf_op jit(solution)/shard_map/dynamic_slice | solution.py:258
  9.3 1.3 collective-permute-done.near
  10.5 6.4 %collective-permute-done.2.cross = bf16[128,512]{1,0:T(8,128)(2,1)S(1)} collective-permute-done((bf16[128,512]{1,0:T(8,128)(2,1)}, bf16[128,512]{1,0:T(8,128)(2,1)S(1)}, u32[]{:S(2)}, u32[]{:S(2)}) %collective-permute-start.2) | collective-permute-done | bytes 131104 | tf_op jit(solution)/shard_map/ppermute | solution.py:34
  16.9 1.0 pack.1
  18.0 0.9 collective-permute-start.22
  18.9 1.3 collective-permute-start.4
  20.2 1.6 %collective-permute-start.9 = (bf16[2,32,3328]{2,1,0:T(8,128)(2,1)S(1)}, bf16[2,32,3328]{2,1,0:T(8,128)(2,1)S(1)}, u32[]{:S(2)}, u32[]{:S(2)}) collective-permute-start(bf16[2,32,3328]{2,1,0:T(8,128)(2,1)S(1)} %get-tuple-element.32.refs_0_), channel_id=1, source_target_pairs={{0,4},{1,5},{2,6},{3,7},{4,0},{5,1},{6,2},{7,3},{8,12},{9,13},{10,... | collective-permute-start | bytes 1277960 | tf_op jit(solution)/shard_map/ppermute | solution.py:41
  21.8 4.7 %collective-permute-start.7 = (bf16[2,32,3328]{2,1,0:T(8,128)(2,1)S(1)}, bf16[2,32,3328]{2,1,0:T(8,128)(2,1)S(1)}, u32[]{:S(2)}, u32[]{:S(2)}) collective-permute-start(bf16[2,32,3328]{2,1,0:T(8,128)(2,1)S(1)} %get-tuple-element.32.refs_0_), channel_id=1, source_target_pairs={{0,28},{1,29},{2,30},{3,31},{4,8},{5,9},{6,10},{7,11},{8,4},{9,5},... | collective-permute-start | bytes 1277960 | tf_op jit(solution)/shard_map/ppermute | solution.py:41
  26.5 1.9 %collective-permute-start.5 = (bf16[2,2,128,512]{3,2,1,0:T(8,128)(2,1)S(1)}, bf16[2,2,128,512]{3,2,1,0:T(8,128)(2,1)S(1)}, u32[]{:S(2)}, u32[]{:S(2)}) collective-permute-start(bf16[2,2,128,512]{3,2,1,0:T(8,128)(2,1)S(1)} %get-tuple-element.31.p0), channel_id=1, source_target_pairs={{0,96},{32,64},{64,32},{96,0},{128,224},{160,192},{192,160},{224,1... | collective-permute-start | bytes 1572872 | tf_op jit(solution)/shard_map/ppermute | solution.py:25
  28.4 2.1 %collective-permute-done.4.p1 = bf16[2,2,128,512]{3,2,1,0:T(8,128)(2,1)S(1)} collective-permute-done((bf16[2,2,128,512]{3,2,1,0:T(8,128)(2,1)S(1)}, bf16[2,2,128,512]{3,2,1,0:T(8,128)(2,1)S(1)}, u32[]{:S(2)}, u32[]{:S(2)}) %collective-permute-start.4) | collective-permute-done | bytes 524320 | tf_op jit(solution)/shard_map/ppermute | solution.py:25
  30.5 2.7 %collective-permute-start.6 = (bf16[2,2,128,512]{3,2,1,0:T(8,128)(2,1)S(1)}, bf16[2,2,128,512]{3,2,1,0:T(8,128)(2,1)S(1)}, u32[]{:S(2)}, u32[]{:S(2)}) collective-permute-start(bf16[2,2,128,512]{3,2,1,0:T(8,128)(2,1)S(1)} %collective-permute-done.4.p1), channel_id=1, source_target_pairs={{0,96},{32,64},{64,32},{96,0},{128,224},{160,192},{192,160},{224,1... | collective-permute-start | bytes 1572872 | tf_op jit(solution)/shard_map/ppermute | solution.py:25
  33.2 5.6 %collective-permute-start.10 = (bf16[2,32,3328]{2,1,0:T(8,128)(2,1)S(1)}, bf16[2,32,3328]{2,1,0:T(8,128)(2,1)S(1)}, u32[]{:S(2)}, u32[]{:S(2)}) collective-permute-start(bf16[2,32,3328]{2,1,0:T(8,128)(2,1)S(1)} %collective-permute-done.9.refs_1_), channel_id=1, source_target_pairs={{0,28},{1,29},{2,30},{3,31},{4,8},{5,9},{6,10},{7,11},{8,4},{9,5},... | collective-permute-start | bytes 1277960 | tf_op jit(solution)/shard_map/ppermute | solution.py:41
  38.8 7.1 %collective-permute-done.10.refs_1_.refs_5_ = bf16[2,32,3328]{2,1,0:T(8,128)(2,1)S(1)} collective-permute-done((bf16[2,32,3328]{2,1,0:T(8,128)(2,1)S(1)}, bf16[2,32,3328]{2,1,0:T(8,128)(2,1)S(1)}, u32[]{:S(2)}, u32[]{:S(2)}) %collective-permute-start.10) | collective-permute-done | bytes 426016 | tf_op jit(solution)/shard_map/ppermute | solution.py:41
  45.9 0.9 collective-permute-done.8.refs_0_.refs_2_
  46.8 1.5 %collective-permute-start.12 = (bf16[2,32,3328]{2,1,0:T(8,128)(2,1)S(1)}, bf16[2,32,3328]{2,1,0:T(8,128)(2,1)S(1)}, u32[]{:S(2)}, u32[]{:S(2)}) collective-permute-start(bf16[2,32,3328]{2,1,0:T(8,128)(2,1)S(1)} %collective-permute-done.8.refs_0_.refs_2_), channel_id=1, source_target_pairs={{0,28},{1,29},{2,30},{3,31},{4,8},{5,9},{6,10},{7,11},{8,4},{9,5},... | collective-permute-start | bytes 1277960 | tf_op jit(solution)/shard_map/ppermute | solution.py:41
  48.3 1.4 %collective-permute-done.6.p3 = bf16[2,2,128,512]{3,2,1,0:T(8,128)(2,1)S(1)} collective-permute-done((bf16[2,2,128,512]{3,2,1,0:T(8,128)(2,1)S(1)}, bf16[2,2,128,512]{3,2,1,0:T(8,128)(2,1)S(1)}, u32[]{:S(2)}, u32[]{:S(2)}) %collective-permute-start.6) | collective-permute-done | bytes 524320 | tf_op jit(solution)/shard_map/ppermute | solution.py:25
  50.4 7.2 %collective-permute-done.11.refs_3_.refs_0_ = bf16[2,32,3328]{2,1,0:T(8,128)(2,1)S(1)} collective-permute-done((bf16[2,32,3328]{2,1,0:T(8,128)(2,1)S(1)}, bf16[2,32,3328]{2,1,0:T(8,128)(2,1)S(1)}, u32[]{:S(2)}, u32[]{:S(2)}) %collective-permute-start.11) | collective-permute-done | bytes 426016 | tf_op jit(solution)/shard_map/ppermute | solution.py:41
  57.6 2.7 %mate_sums.1 = (f32[3,832,128]{2,1,0:T(8,128)S(1)}, f32[5,832,128]{2,1,0:T(8,128)S(1)}) custom-call(s32[13]{0:T(128)S(1)} %stack.64.where, bf16[3328,512]{1,0:T(8,128)(2,1)S(1)} %copy-done, bf16[1664,512]{1,0:T(8,128)(2,1)S(1)} %collective-permute-done.22.got, bf16[8,128,1024]{2,1,0:T(8,128)(2,1)S(1)} %rows.1, ...), custom_call_target="tpu_custom_call" | custom-call | flops 1744830464 | bytes 1048576 | tf_op jit(solution)/shard_map/mate_sums/pallas_call | solution.py:50
  60.3 4.8 %collective-permute-start.23 = (f32[5,832,128]{2,1,0:T(8,128)S(1)}, f32[5,832,128]{2,1,0:T(8,128)S(1)}, u32[]{:S(2)}, u32[]{:S(2)}) collective-permute-start(f32[5,832,128]{2,1,0:T(8,128)S(1)} %get-tuple-element.35), channel_id=1, source_target_pairs={{0,1},{1,0},{2,3},{3,2},{4,5},{5,4},{6,7},{7,6},{8,9},{9,8},{10,11... | collective-permute-start | bytes 6389768 | tf_op jit(solution)/shard_map/ppermute | solution.py:21
  65.4 2.7 %own_sums.1.own = f32[8,832,128]{2,1,0:T(8,128)S(1)} custom-call(s32[13]{0:T(128)S(1)} %stack.64.where, bf16[3328,512]{1,0:T(8,128)(2,1)S(1)} %copy-done, bf16[1664,512]{1,0:T(8,128)(2,1)S(1)} %collective-permute-done.22.got, bf16[8,128,1024]{2,1,0:T(8,128)(2,1)S(1)} %rows.1), custom_call_target="tpu_custom_call" | custom-call | flops 1744830464 | bytes 1048576 | tf_op jit(solution)/shard_map/own_sums/pallas_call | solution.py:50
  68.1 2.7 %collective-permute-done.24.first = f32[3,832,128]{2,1,0:T(8,128)S(1)} collective-permute-done((f32[3,832,128]{2,1,0:T(8,128)S(1)}, f32[3,832,128]{2,1,0:T(8,128)S(1)}, u32[]{:S(2)}, u32[]{:S(2)}) %collective-permute-start.24) | collective-permute-done | bytes 1277984 | tf_op jit(solution)/shard_map/ppermute | solution.py:21
  70.9 1.4 %collective-permute-start.34 = (f32[208,128]{1,0:T(8,128)S(1)}, f32[208,128]{1,0:T(8,128)S(1)}, u32[]{:S(2)}, u32[]{:S(2)}) collective-permute-start(f32[208,128]{1,0:T(8,128)S(1)} %get-tuple-element.49), channel_id=1, source_target_pairs={{0,28},{1,29},{2,30},{3,31},{4,8},{5,9},{6,10},{7,11},{8,4},{9,5},... | collective-permute-start | bytes 319496 | tf_op jit(solution)/shard_map/ppermute | solution.py:41
  72.3 1.0 collective-permute-start.25
  73.9 1.2 collective-permute-done.33.came_left
  75.1 2.0 %collective-permute-start.14 = (bf16[2,32,3328]{2,1,0:T(8,128)(2,1)S(1)}, bf16[2,32,3328]{2,1,0:T(8,128)(2,1)S(1)}, u32[]{:S(2)}, u32[]{:S(2)}) collective-permute-start(bf16[2,32,3328]{2,1,0:T(8,128)(2,1)S(1)} %get-tuple-element.32.refs_0_), channel_id=1, source_target_pairs={{0,1},{1,0},{2,3},{3,2},{4,5},{5,4},{6,7},{7,6},{8,9},{9,8},{10,11... | collective-permute-start | bytes 1277960 | tf_op jit(solution)/shard_map/ppermute | solution.py:21
  77.6 1.0 collective-permute-start.18
  79.1 1.2 collective-permute-start.27
  80.3 1.2 collective-permute-start.28
  81.5 6.6 %collective-permute-done.13.refs_7_ = bf16[2,32,3328]{2,1,0:T(8,128)(2,1)S(1)} collective-permute-done((bf16[2,32,3328]{2,1,0:T(8,128)(2,1)S(1)}, bf16[2,32,3328]{2,1,0:T(8,128)(2,1)S(1)}, u32[]{:S(2)}, u32[]{:S(2)}) %collective-permute-start.13) | collective-permute-done | bytes 426016 | tf_op jit(solution)/shard_map/ppermute | solution.py:41
  88.0 1.6 %collective-permute-start.36 = (f32[416,128]{1,0:T(8,128)S(1)}, f32[416,128]{1,0:T(8,128)S(1)}, u32[]{:S(2)}, u32[]{:S(2)}) collective-permute-start(f32[416,128]{1,0:T(8,128)S(1)} %get-tuple-element.51), channel_id=1, source_target_pairs={{0,28},{1,29},{2,30},{3,31},{4,8},{5,9},{6,10},{7,11},{8,4},{9,5},... | collective-permute-start | bytes 638984 | tf_op jit(solution)/shard_map/ppermute | solution.py:41
  89.6 3.0 %collective-permute-done.27.came_left = f32[416,128]{1,0:T(8,128)S(1)} collective-permute-done((f32[416,128]{1,0:T(8,128)S(1)}, f32[416,128]{1,0:T(8,128)S(1)}, u32[]{:S(2)}, u32[]{:S(2)}) %collective-permute-start.27) | collective-permute-done | bytes 213024 | tf_op jit(solution)/shard_map/ppermute | solution.py:41
  92.6 5.1 %collective-permute-start.19 = (bf16[2,32,3328]{2,1,0:T(8,128)(2,1)S(1)}, bf16[2,32,3328]{2,1,0:T(8,128)(2,1)S(1)}, u32[]{:S(2)}, u32[]{:S(2)}) collective-permute-start(bf16[2,32,3328]{2,1,0:T(8,128)(2,1)S(1)} %collective-permute-done.10.refs_1_.refs_5_), channel_id=1, source_target_pairs={{0,1},{1,0},{2,3},{3,2},{4,5},{5,4},{6,7},{7,6},{8,9},{9,8},{10,11... | collective-permute-start | bytes 1277960 | tf_op jit(solution)/shard_map/ppermute | solution.py:21
  97.7 2.3 %collective-permute-start.17 = (bf16[2,32,3328]{2,1,0:T(8,128)(2,1)S(1)}, bf16[2,32,3328]{2,1,0:T(8,128)(2,1)S(1)}, u32[]{:S(2)}, u32[]{:S(2)}) collective-permute-start(bf16[2,32,3328]{2,1,0:T(8,128)(2,1)S(1)} %collective-permute-done.11.refs_3_.refs_0_), channel_id=1, source_target_pairs={{0,1},{1,0},{2,3},{3,2},{4,5},{5,4},{6,7},{7,6},{8,9},{9,8},{10,11... | collective-permute-start | bytes 1277960 | tf_op jit(solution)/shard_map/ppermute | solution.py:21
  101.2 1.1 collective-permute-start.38
  103.1 1.1 collective-permute-start.30
  104.2 5.3 %weight_sum.1 = (bf16[3328,512]{1,0:T(8,128)(2,1)}, bf16[16,128]{1,0:T(8,128)(2,1)S(1)}) custom-call(s32[13]{0:T(128)S(1)} %stack.64.where, bf16[8,128,1024]{2,1,0:T(8,128)(2,1)S(1)} %rows.1, bf16[2,32,3328]{2,1,0:T(8,128)(2,1)S(1)} %get-tuple-element.32.refs_0_, bf16[2,32,3328]{2,1,0:T(8,128)(2,1)S(1)} %collective-permute-done.9.refs_1_, ...), custom_call_target="tpu_custom_call" | custom-call | flops 3489660928 | bytes 1048576 | tf_op jit(solution)/shard_map/weight_sum/pallas_call | solution.py:50
  109.9 1.6 %collective-permute-start.40 = (f32[416,128]{1,0:T(8,128)S(1)}, f32[416,128]{1,0:T(8,128)S(1)}, u32[]{:S(2)}, u32[]{:S(2)}) collective-permute-start(f32[416,128]{1,0:T(8,128)S(1)} %get-tuple-element.59), channel_id=1, source_target_pairs={{0,28},{1,29},{2,30},{3,31},{4,8},{5,9},{6,10},{7,11},{8,4},{9,5},... | collective-permute-start | bytes 638984 | tf_op jit(solution)/shard_map/ppermute | solution.py:41
  111.9 1.5 %collective-permute-done.30.came_right = f32[416,128]{1,0:T(8,128)S(1)} collective-permute-done((f32[416,128]{1,0:T(8,128)S(1)}, f32[416,128]{1,0:T(8,128)S(1)}, u32[]{:S(2)}, u32[]{:S(2)}) %collective-permute-start.30) | collective-permute-done | bytes 213024 | tf_op jit(solution)/shard_map/ppermute | solution.py:41
  113.6 1.3 collective-permute-start.32
  115.6 1.6 %collective-permute-done.40.refs_5_ = f32[416,128]{1,0:T(8,128)S(1)} collective-permute-done((f32[416,128]{1,0:T(8,128)S(1)}, f32[416,128]{1,0:T(8,128)S(1)}, u32[]{:S(2)}, u32[]{:S(2)}) %collective-permute-start.40) | collective-permute-done | bytes 213024 | tf_op jit(solution)/shard_map/ppermute | solution.py:41
  117.2 3.4 %collective-permute-done.31.refs_1_ = f32[416,128]{1,0:T(8,128)S(1)} collective-permute-done((f32[416,128]{1,0:T(8,128)S(1)}, f32[416,128]{1,0:T(8,128)S(1)}, u32[]{:S(2)}, u32[]{:S(2)}) %collective-permute-start.31) | collective-permute-done | bytes 213024 | tf_op jit(solution)/shard_map/ppermute | solution.py:41
  120.6 1.6 %collective-permute-done.32.refs_2_ = f32[416,128]{1,0:T(8,128)S(1)} collective-permute-done((f32[416,128]{1,0:T(8,128)S(1)}, f32[416,128]{1,0:T(8,128)S(1)}, u32[]{:S(2)}, u32[]{:S(2)}) %collective-permute-start.32) | collective-permute-done | bytes 213024 | tf_op jit(solution)/shard_map/ppermute | solution.py:41
  122.5 2.4 %collective-permute-start.41 = (bf16[64,832]{1,0:T(8,128)(2,1)S(1)}, bf16[64,832]{1,0:T(8,128)(2,1)S(1)}, u32[]{:S(2)}, u32[]{:S(2)}) collective-permute-start(bf16[64,832]{1,0:T(8,128)(2,1)S(1)} %dynamic-slice_bitcast_fusion), channel_id=1, source_target_pairs={{0,2},{1,3},{2,0},{3,1},{4,6},{5,7},{6,4},{7,5},{8,10},{9,11},{10,... | collective-permute-start | bytes 319496 | tf_op jit(solution)/shard_map/ppermute | solution.py:21
  125.0 2.8 %collective-permute-done.41 = bf16[64,832]{1,0:T(8,128)(2,1)S(1)} collective-permute-done((bf16[64,832]{1,0:T(8,128)(2,1)S(1)}, bf16[64,832]{1,0:T(8,128)(2,1)S(1)}, u32[]{:S(2)}, u32[]{:S(2)}) %collective-permute-start.41) | collective-permute-done | bytes 106528 | tf_op jit(solution)/shard_map/ppermute | solution.py:21
  127.8 2.8 %collective-permute-start.42 = (bf16[2,32,832]{2,1,0:T(8,128)(2,1)S(1)}, bf16[2,32,832]{2,1,0:T(8,128)(2,1)S(1)}, u32[]{:S(2)}, u32[]{:S(2)}) collective-permute-start(bf16[2,32,832]{2,1,0:T(8,128)(2,1)S(1)} %fusion.1), channel_id=1, source_target_pairs={{0,1},{1,0},{2,3},{3,2},{4,5},{5,4},{6,7},{7,6},{8,9},{9,8},{10,11... | collective-permute-start | bytes 319496 | tf_op jit(solution)/shard_map/ppermute | solution.py:21
  130.6 1.0 collective-permute-done.42
  (68 shorter events, 8.6 us)
Async XLA Ops:
  0.6 16.3 %copy-start.2 = (bf16[128,512]{1,0:T(8,128)(2,1)S(1)}, bf16[128,512]{1,0:T(8,128)(2,1)}, u32[]{:S(2)}) copy-start(bf16[128,512]{1,0:T(8,128)(2,1)} %own.1) | copy-start | bytes 393220
  0.6 16.3 %copy-start.1 = (bf16[32,3328]{1,0:T(8,128)(2,1)S(1)}, bf16[32,3328]{1,0:T(8,128)(2,1)}, u32[]{:S(2)}) copy-start(bf16[32,3328]{1,0:T(8,128)(2,1)} %hidden.1) | copy-start | bytes 638980
  0.6 8.6 %collective-permute-start.1 = (bf16[128,512]{1,0:T(8,128)(2,1)}, bf16[128,512]{1,0:T(8,128)(2,1)S(1)}, u32[]{:S(2)}, u32[]{:S(2)}) collective-permute-start(bf16[128,512]{1,0:T(8,128)(2,1)} %own.1), channel_id=1, source_target_pairs={{0,2},{1,3},{2,0},{3,1},{4,6},{5,7},{6,4},{7,5},{8,10},{9,11},{10,... | collective-permute-start | bytes 393224 | tf_op jit(solution)/shard_map/ppermute | solution.py:21
  4.3 6.2 %collective-permute-start = (bf16[128,512]{1,0:T(8,128)(2,1)}, bf16[128,512]{1,0:T(8,128)(2,1)S(1)}, u32[]{:S(2)}, u32[]{:S(2)}) collective-permute-start(bf16[128,512]{1,0:T(8,128)(2,1)} %own.1), channel_id=1, source_target_pairs={{0,128},{32,160},{64,192},{96,224},{128,0},{160,32},{192,64},{224,... | collective-permute-start | bytes 393224 | tf_op jit(solution)/shard_map/ppermute | solution.py:25
  4.6 12.3 %collective-permute-start.2 = (bf16[128,512]{1,0:T(8,128)(2,1)}, bf16[128,512]{1,0:T(8,128)(2,1)S(1)}, u32[]{:S(2)}, u32[]{:S(2)}) collective-permute-start(bf16[128,512]{1,0:T(8,128)(2,1)} %own.1), channel_id=1, source_target_pairs={{0,130},{1,131},{2,128},{3,129},{4,134},{5,135},{6,132},{7,133},{8... | collective-permute-start | bytes 393224 | tf_op jit(solution)/shard_map/ppermute | solution.py:34
  5.2 11.7 %collective-permute-start.3 = (bf16[32,3328]{1,0:T(8,128)(2,1)}, bf16[32,3328]{1,0:T(8,128)(2,1)S(1)}, u32[]{:S(2)}, u32[]{:S(2)}) collective-permute-start(bf16[32,3328]{1,0:T(8,128)(2,1)} %hidden.1), channel_id=1, source_target_pairs={{0,2},{1,3},{2,0},{3,1},{4,6},{5,7},{6,4},{7,5},{8,10},{9,11},{10,... | collective-permute-start | bytes 638984 | tf_op jit(solution)/shard_map/ppermute | solution.py:21
  18.0 39.7 %collective-permute-start.22 = (bf16[1664,512]{1,0:T(8,128)(2,1)S(1)}, bf16[1664,512]{1,0:T(8,128)(2,1)S(1)}, u32[]{:S(2)}, u32[]{:S(2)}) collective-permute-start(bf16[1664,512]{1,0:T(8,128)(2,1)S(1)} %get-tuple-element.34), channel_id=1, source_target_pairs={{0,2},{1,3},{2,0},{3,1},{4,6},{5,7},{6,4},{7,5},{8,10},{9,11},{10,... | collective-permute-start | bytes 5111816 | tf_op jit(solution)/shard_map/ppermute | solution.py:21
  18.9 11.6 %collective-permute-start.4 = (bf16[2,2,128,512]{3,2,1,0:T(8,128)(2,1)S(1)}, bf16[2,2,128,512]{3,2,1,0:T(8,128)(2,1)S(1)}, u32[]{:S(2)}, u32[]{:S(2)}) collective-permute-start(bf16[2,2,128,512]{3,2,1,0:T(8,128)(2,1)S(1)} %get-tuple-element.31.p0), channel_id=1, source_target_pairs={{0,32},{32,0},{64,96},{96,64},{128,160},{160,128},{192,224},{224,1... | collective-permute-start | bytes 1572872 | tf_op jit(solution)/shard_map/ppermute | solution.py:25
  20.2 37.4 %copy-start = (bf16[3328,512]{1,0:T(8,128)(2,1)S(1)}, bf16[3328,512]{1,0:T(8,128)(2,1)}, u32[]{:S(2)}) copy-start(bf16[3328,512]{1,0:T(8,128)(2,1)} %down.3) | copy-start | bytes 10223620
  20.2 13.0 %collective-permute-start.9 = (bf16[2,32,3328]{2,1,0:T(8,128)(2,1)S(1)}, bf16[2,32,3328]{2,1,0:T(8,128)(2,1)S(1)}, u32[]{:S(2)}, u32[]{:S(2)}) collective-permute-start(bf16[2,32,3328]{2,1,0:T(8,128)(2,1)S(1)} %get-tuple-element.32.refs_0_), channel_id=1, source_target_pairs={{0,4},{1,5},{2,6},{3,7},{4,0},{5,1},{6,2},{7,3},{8,12},{9,13},{10,... | collective-permute-start | bytes 1277960 | tf_op jit(solution)/shard_map/ppermute | solution.py:41
  21.8 17.0 %collective-permute-start.7 = (bf16[2,32,3328]{2,1,0:T(8,128)(2,1)S(1)}, bf16[2,32,3328]{2,1,0:T(8,128)(2,1)S(1)}, u32[]{:S(2)}, u32[]{:S(2)}) collective-permute-start(bf16[2,32,3328]{2,1,0:T(8,128)(2,1)S(1)} %get-tuple-element.32.refs_0_), channel_id=1, source_target_pairs={{0,28},{1,29},{2,30},{3,31},{4,8},{5,9},{6,10},{7,11},{8,4},{9,5},... | collective-permute-start | bytes 1277960 | tf_op jit(solution)/shard_map/ppermute | solution.py:41
  26.5 21.8 %collective-permute-start.5 = (bf16[2,2,128,512]{3,2,1,0:T(8,128)(2,1)S(1)}, bf16[2,2,128,512]{3,2,1,0:T(8,128)(2,1)S(1)}, u32[]{:S(2)}, u32[]{:S(2)}) collective-permute-start(bf16[2,2,128,512]{3,2,1,0:T(8,128)(2,1)S(1)} %get-tuple-element.31.p0), channel_id=1, source_target_pairs={{0,96},{32,64},{64,32},{96,0},{128,224},{160,192},{192,160},{224,1... | collective-permute-start | bytes 1572872 | tf_op jit(solution)/shard_map/ppermute | solution.py:25
  30.5 19.2 %collective-permute-start.6 = (bf16[2,2,128,512]{3,2,1,0:T(8,128)(2,1)S(1)}, bf16[2,2,128,512]{3,2,1,0:T(8,128)(2,1)S(1)}, u32[]{:S(2)}, u32[]{:S(2)}) collective-permute-start(bf16[2,2,128,512]{3,2,1,0:T(8,128)(2,1)S(1)} %collective-permute-done.4.p1), channel_id=1, source_target_pairs={{0,96},{32,64},{64,32},{96,0},{128,224},{160,192},{192,160},{224,1... | collective-permute-start | bytes 1572872 | tf_op jit(solution)/shard_map/ppermute | solution.py:25
  33.2 12.7 %collective-permute-start.10 = (bf16[2,32,3328]{2,1,0:T(8,128)(2,1)S(1)}, bf16[2,32,3328]{2,1,0:T(8,128)(2,1)S(1)}, u32[]{:S(2)}, u32[]{:S(2)}) collective-permute-start(bf16[2,32,3328]{2,1,0:T(8,128)(2,1)S(1)} %collective-permute-done.9.refs_1_), channel_id=1, source_target_pairs={{0,28},{1,29},{2,30},{3,31},{4,8},{5,9},{6,10},{7,11},{8,4},{9,5},... | collective-permute-start | bytes 1277960 | tf_op jit(solution)/shard_map/ppermute | solution.py:41
  38.8 8.0 %collective-permute-start.8 = (bf16[2,32,3328]{2,1,0:T(8,128)(2,1)S(1)}, bf16[2,32,3328]{2,1,0:T(8,128)(2,1)S(1)}, u32[]{:S(2)}, u32[]{:S(2)}) collective-permute-start(bf16[2,32,3328]{2,1,0:T(8,128)(2,1)S(1)} %collective-permute-done.7.refs_4_), channel_id=1, source_target_pairs={{0,4},{1,5},{2,6},{3,7},{4,0},{5,1},{6,2},{7,3},{8,12},{9,13},{10,... | collective-permute-start | bytes 1277960 | tf_op jit(solution)/shard_map/ppermute | solution.py:41
  45.9 11.7 %collective-permute-start.11 = (bf16[2,32,3328]{2,1,0:T(8,128)(2,1)S(1)}, bf16[2,32,3328]{2,1,0:T(8,128)(2,1)S(1)}, u32[]{:S(2)}, u32[]{:S(2)}) collective-permute-start(bf16[2,32,3328]{2,1,0:T(8,128)(2,1)S(1)} %collective-permute-done.10.refs_1_.refs_5_), channel_id=1, source_target_pairs={{0,4},{1,5},{2,6},{3,7},{4,0},{5,1},{6,2},{7,3},{8,12},{9,13},{10,... | collective-permute-start | bytes 1277960 | tf_op jit(solution)/shard_map/ppermute | solution.py:41
  46.8 10.8 %collective-permute-start.12 = (bf16[2,32,3328]{2,1,0:T(8,128)(2,1)S(1)}, bf16[2,32,3328]{2,1,0:T(8,128)(2,1)S(1)}, u32[]{:S(2)}, u32[]{:S(2)}) collective-permute-start(bf16[2,32,3328]{2,1,0:T(8,128)(2,1)S(1)} %collective-permute-done.8.refs_0_.refs_2_), channel_id=1, source_target_pairs={{0,28},{1,29},{2,30},{3,31},{4,8},{5,9},{6,10},{7,11},{8,4},{9,5},... | collective-permute-start | bytes 1277960 | tf_op jit(solution)/shard_map/ppermute | solution.py:41
  60.3 39.9 %collective-permute-start.23 = (f32[5,832,128]{2,1,0:T(8,128)S(1)}, f32[5,832,128]{2,1,0:T(8,128)S(1)}, u32[]{:S(2)}, u32[]{:S(2)}) collective-permute-start(f32[5,832,128]{2,1,0:T(8,128)S(1)} %get-tuple-element.35), channel_id=1, source_target_pairs={{0,1},{1,0},{2,3},{3,2},{4,5},{5,4},{6,7},{7,6},{8,9},{9,8},{10,11... | collective-permute-start | bytes 6389768 | tf_op jit(solution)/shard_map/ppermute | solution.py:21
  65.1 5.7 %collective-permute-start.24 = (f32[3,832,128]{2,1,0:T(8,128)S(1)}, f32[3,832,128]{2,1,0:T(8,128)S(1)}, u32[]{:S(2)}, u32[]{:S(2)}) collective-permute-start(f32[3,832,128]{2,1,0:T(8,128)S(1)} %get-tuple-element.36), channel_id=1, source_target_pairs={{0,1},{1,0},{2,3},{3,2},{4,5},{5,4},{6,7},{7,6},{8,9},{9,8},{10,11... | collective-permute-start | bytes 3833864 | tf_op jit(solution)/shard_map/ppermute | solution.py:21
  70.8 4.3 %collective-permute-start.33 = (f32[208,128]{1,0:T(8,128)S(1)}, f32[208,128]{1,0:T(8,128)S(1)}, u32[]{:S(2)}, u32[]{:S(2)}) collective-permute-start(f32[208,128]{1,0:T(8,128)S(1)} %get-tuple-element.48), channel_id=1, source_target_pairs={{0,4},{1,5},{2,6},{3,7},{4,0},{5,1},{6,2},{7,3},{8,12},{9,13},{10,... | collective-permute-start | bytes 319496 | tf_op jit(solution)/shard_map/ppermute | solution.py:41
  70.9 6.2 %collective-permute-start.34 = (f32[208,128]{1,0:T(8,128)S(1)}, f32[208,128]{1,0:T(8,128)S(1)}, u32[]{:S(2)}, u32[]{:S(2)}) collective-permute-start(f32[208,128]{1,0:T(8,128)S(1)} %get-tuple-element.49), channel_id=1, source_target_pairs={{0,28},{1,29},{2,30},{3,31},{4,8},{5,9},{6,10},{7,11},{8,4},{9,5},... | collective-permute-start | bytes 319496 | tf_op jit(solution)/shard_map/ppermute | solution.py:41
  72.3 5.3 %collective-permute-start.25 = (f32[208,128]{1,0:T(8,128)S(1)}, f32[208,128]{1,0:T(8,128)S(1)}, u32[]{:S(2)}, u32[]{:S(2)}) collective-permute-start(f32[208,128]{1,0:T(8,128)S(1)} %get-tuple-element.37), channel_id=1, source_target_pairs={{0,4},{1,5},{2,6},{3,7},{4,0},{5,1},{6,2},{7,3},{8,12},{9,13},{10,... | collective-permute-start | bytes 319496 | tf_op jit(solution)/shard_map/ppermute | solution.py:41
  73.3 5.3 %collective-permute-start.26 = (f32[208,128]{1,0:T(8,128)S(1)}, f32[208,128]{1,0:T(8,128)S(1)}, u32[]{:S(2)}, u32[]{:S(2)}) collective-permute-start(f32[208,128]{1,0:T(8,128)S(1)} %get-tuple-element.38), channel_id=1, source_target_pairs={{0,28},{1,29},{2,30},{3,31},{4,8},{5,9},{6,10},{7,11},{8,4},{9,5},... | collective-permute-start | bytes 319496 | tf_op jit(solution)/shard_map/ppermute | solution.py:41
  75.1 4.0 %collective-permute-start.14 = (bf16[2,32,3328]{2,1,0:T(8,128)(2,1)S(1)}, bf16[2,32,3328]{2,1,0:T(8,128)(2,1)S(1)}, u32[]{:S(2)}, u32[]{:S(2)}) collective-permute-start(bf16[2,32,3328]{2,1,0:T(8,128)(2,1)S(1)} %get-tuple-element.32.refs_0_), channel_id=1, source_target_pairs={{0,1},{1,0},{2,3},{3,2},{4,5},{5,4},{6,7},{7,6},{8,9},{9,8},{10,11... | collective-permute-start | bytes 1277960 | tf_op jit(solution)/shard_map/ppermute | solution.py:21
  77.1 3.2 %collective-permute-start.15 = (bf16[2,32,3328]{2,1,0:T(8,128)(2,1)S(1)}, bf16[2,32,3328]{2,1,0:T(8,128)(2,1)S(1)}, u32[]{:S(2)}, u32[]{:S(2)}) collective-permute-start(bf16[2,32,3328]{2,1,0:T(8,128)(2,1)S(1)} %collective-permute-done.9.refs_1_), channel_id=1, source_target_pairs={{0,1},{1,0},{2,3},{3,2},{4,5},{5,4},{6,7},{7,6},{8,9},{9,8},{10,11... | collective-permute-start | bytes 1277960 | tf_op jit(solution)/shard_map/ppermute | solution.py:21
  77.6 3.9 %collective-permute-start.18 = (bf16[2,32,3328]{2,1,0:T(8,128)(2,1)S(1)}, bf16[2,32,3328]{2,1,0:T(8,128)(2,1)S(1)}, u32[]{:S(2)}, u32[]{:S(2)}) collective-permute-start(bf16[2,32,3328]{2,1,0:T(8,128)(2,1)S(1)} %collective-permute-done.7.refs_4_), channel_id=1, source_target_pairs={{0,1},{1,0},{2,3},{3,2},{4,5},{5,4},{6,7},{7,6},{8,9},{9,8},{10,11... | collective-permute-start | bytes 1277960 | tf_op jit(solution)/shard_map/ppermute | solution.py:21
  78.6 9.5 %collective-permute-start.13 = (bf16[2,32,3328]{2,1,0:T(8,128)(2,1)S(1)}, bf16[2,32,3328]{2,1,0:T(8,128)(2,1)S(1)}, u32[]{:S(2)}, u32[]{:S(2)}) collective-permute-start(bf16[2,32,3328]{2,1,0:T(8,128)(2,1)S(1)} %collective-permute-done.12.refs_6_.refs_1_), channel_id=1, source_target_pairs={{0,4},{1,5},{2,6},{3,7},{4,0},{5,1},{6,2},{7,3},{8,12},{9,13},{10,... | collective-permute-start | bytes 1277960 | tf_op jit(solution)/shard_map/ppermute | solution.py:41
  79.1 13.5 %collective-permute-start.27 = (f32[416,128]{1,0:T(8,128)S(1)}, f32[416,128]{1,0:T(8,128)S(1)}, u32[]{:S(2)}, u32[]{:S(2)}) collective-permute-start(f32[416,128]{1,0:T(8,128)S(1)} %get-tuple-element.39), channel_id=1, source_target_pairs={{0,4},{1,5},{2,6},{3,7},{4,0},{5,1},{6,2},{7,3},{8,12},{9,13},{10,... | collective-permute-start | bytes 638984 | tf_op jit(solution)/shard_map/ppermute | solution.py:41
  80.3 17.4 %collective-permute-start.28 = (f32[416,128]{1,0:T(8,128)S(1)}, f32[416,128]{1,0:T(8,128)S(1)}, u32[]{:S(2)}, u32[]{:S(2)}) collective-permute-start(f32[416,128]{1,0:T(8,128)S(1)} %get-tuple-element.40), channel_id=1, source_target_pairs={{0,28},{1,29},{2,30},{3,31},{4,8},{5,9},{6,10},{7,11},{8,4},{9,5},... | collective-permute-start | bytes 638984 | tf_op jit(solution)/shard_map/ppermute | solution.py:41
  81.5 16.2 %collective-permute-start.35 = (f32[416,128]{1,0:T(8,128)S(1)}, f32[416,128]{1,0:T(8,128)S(1)}, u32[]{:S(2)}, u32[]{:S(2)}) collective-permute-start(f32[416,128]{1,0:T(8,128)S(1)} %get-tuple-element.50), channel_id=1, source_target_pairs={{0,4},{1,5},{2,6},{3,7},{4,0},{5,1},{6,2},{7,3},{8,12},{9,13},{10,... | collective-permute-start | bytes 638984 | tf_op jit(solution)/shard_map/ppermute | solution.py:41
  88.0 11.9 %collective-permute-start.36 = (f32[416,128]{1,0:T(8,128)S(1)}, f32[416,128]{1,0:T(8,128)S(1)}, u32[]{:S(2)}, u32[]{:S(2)}) collective-permute-start(f32[416,128]{1,0:T(8,128)S(1)} %get-tuple-element.51), channel_id=1, source_target_pairs={{0,28},{1,29},{2,30},{3,31},{4,8},{5,9},{6,10},{7,11},{8,4},{9,5},... | collective-permute-start | bytes 638984 | tf_op jit(solution)/shard_map/ppermute | solution.py:41
  92.6 8.1 %collective-permute-start.19 = (bf16[2,32,3328]{2,1,0:T(8,128)(2,1)S(1)}, bf16[2,32,3328]{2,1,0:T(8,128)(2,1)S(1)}, u32[]{:S(2)}, u32[]{:S(2)}) collective-permute-start(bf16[2,32,3328]{2,1,0:T(8,128)(2,1)S(1)} %collective-permute-done.10.refs_1_.refs_5_), channel_id=1, source_target_pairs={{0,1},{1,0},{2,3},{3,2},{4,5},{5,4},{6,7},{7,6},{8,9},{9,8},{10,11... | collective-permute-start | bytes 1277960 | tf_op jit(solution)/shard_map/ppermute | solution.py:21
  97.7 3.6 %collective-permute-start.16 = (bf16[2,32,3328]{2,1,0:T(8,128)(2,1)S(1)}, bf16[2,32,3328]{2,1,0:T(8,128)(2,1)S(1)}, u32[]{:S(2)}, u32[]{:S(2)}) collective-permute-start(bf16[2,32,3328]{2,1,0:T(8,128)(2,1)S(1)} %collective-permute-done.8.refs_0_.refs_2_), channel_id=1, source_target_pairs={{0,1},{1,0},{2,3},{3,2},{4,5},{5,4},{6,7},{7,6},{8,9},{9,8},{10,11... | collective-permute-start | bytes 1277960 | tf_op jit(solution)/shard_map/ppermute | solution.py:21
  97.7 4.7 %collective-permute-start.17 = (bf16[2,32,3328]{2,1,0:T(8,128)(2,1)S(1)}, bf16[2,32,3328]{2,1,0:T(8,128)(2,1)S(1)}, u32[]{:S(2)}, u32[]{:S(2)}) collective-permute-start(bf16[2,32,3328]{2,1,0:T(8,128)(2,1)S(1)} %collective-permute-done.11.refs_3_.refs_0_), channel_id=1, source_target_pairs={{0,1},{1,0},{2,3},{3,2},{4,5},{5,4},{6,7},{7,6},{8,9},{9,8},{10,11... | collective-permute-start | bytes 1277960 | tf_op jit(solution)/shard_map/ppermute | solution.py:21
  99.9 3.2 %collective-permute-start.20 = (bf16[2,32,3328]{2,1,0:T(8,128)(2,1)S(1)}, bf16[2,32,3328]{2,1,0:T(8,128)(2,1)S(1)}, u32[]{:S(2)}, u32[]{:S(2)}) collective-permute-start(bf16[2,32,3328]{2,1,0:T(8,128)(2,1)S(1)} %collective-permute-done.12.refs_6_.refs_1_), channel_id=1, source_target_pairs={{0,1},{1,0},{2,3},{3,2},{4,5},{5,4},{6,7},{7,6},{8,9},{9,8},{10,11... | collective-permute-start | bytes 1277960 | tf_op jit(solution)/shard_map/ppermute | solution.py:21
  100.2 3.9 %collective-permute-start.21 = (bf16[2,32,3328]{2,1,0:T(8,128)(2,1)S(1)}, bf16[2,32,3328]{2,1,0:T(8,128)(2,1)S(1)}, u32[]{:S(2)}, u32[]{:S(2)}) collective-permute-start(bf16[2,32,3328]{2,1,0:T(8,128)(2,1)S(1)} %collective-permute-done.13.refs_7_), channel_id=1, source_target_pairs={{0,1},{1,0},{2,3},{3,2},{4,5},{5,4},{6,7},{7,6},{8,9},{9,8},{10,11... | collective-permute-start | bytes 1277960 | tf_op jit(solution)/shard_map/ppermute | solution.py:21
  100.7 8.7 %collective-permute-start.37 = (f32[416,128]{1,0:T(8,128)S(1)}, f32[416,128]{1,0:T(8,128)S(1)}, u32[]{:S(2)}, u32[]{:S(2)}) collective-permute-start(f32[416,128]{1,0:T(8,128)S(1)} %get-tuple-element.55), channel_id=1, source_target_pairs={{0,4},{1,5},{2,6},{3,7},{4,0},{5,1},{6,2},{7,3},{8,12},{9,13},{10,... | collective-permute-start | bytes 638984 | tf_op jit(solution)/shard_map/ppermute | solution.py:41
  101.2 8.3 %collective-permute-start.38 = (f32[416,128]{1,0:T(8,128)S(1)}, f32[416,128]{1,0:T(8,128)S(1)}, u32[]{:S(2)}, u32[]{:S(2)}) collective-permute-start(f32[416,128]{1,0:T(8,128)S(1)} %get-tuple-element.56), channel_id=1, source_target_pairs={{0,28},{1,29},{2,30},{3,31},{4,8},{5,9},{6,10},{7,11},{8,4},{9,5},... | collective-permute-start | bytes 638984 | tf_op jit(solution)/shard_map/ppermute | solution.py:41
  102.3 9.6 %collective-permute-start.29 = (f32[416,128]{1,0:T(8,128)S(1)}, f32[416,128]{1,0:T(8,128)S(1)}, u32[]{:S(2)}, u32[]{:S(2)}) collective-permute-start(f32[416,128]{1,0:T(8,128)S(1)} %get-tuple-element.44), channel_id=1, source_target_pairs={{0,4},{1,5},{2,6},{3,7},{4,0},{5,1},{6,2},{7,3},{8,12},{9,13},{10,... | collective-permute-start | bytes 638984 | tf_op jit(solution)/shard_map/ppermute | solution.py:41
  103.1 10.3 %collective-permute-start.30 = (f32[416,128]{1,0:T(8,128)S(1)}, f32[416,128]{1,0:T(8,128)S(1)}, u32[]{:S(2)}, u32[]{:S(2)}) collective-permute-start(f32[416,128]{1,0:T(8,128)S(1)} %get-tuple-element.45), channel_id=1, source_target_pairs={{0,28},{1,29},{2,30},{3,31},{4,8},{5,9},{6,10},{7,11},{8,4},{9,5},... | collective-permute-start | bytes 638984 | tf_op jit(solution)/shard_map/ppermute | solution.py:41
  109.5 6.1 %collective-permute-start.39 = (f32[416,128]{1,0:T(8,128)S(1)}, f32[416,128]{1,0:T(8,128)S(1)}, u32[]{:S(2)}, u32[]{:S(2)}) collective-permute-start(f32[416,128]{1,0:T(8,128)S(1)} %get-tuple-element.58), channel_id=1, source_target_pairs={{0,4},{1,5},{2,6},{3,7},{4,0},{5,1},{6,2},{7,3},{8,12},{9,13},{10,... | collective-permute-start | bytes 638984 | tf_op jit(solution)/shard_map/ppermute | solution.py:41
  109.9 7.3 %collective-permute-start.40 = (f32[416,128]{1,0:T(8,128)S(1)}, f32[416,128]{1,0:T(8,128)S(1)}, u32[]{:S(2)}, u32[]{:S(2)}) collective-permute-start(f32[416,128]{1,0:T(8,128)S(1)} %get-tuple-element.59), channel_id=1, source_target_pairs={{0,28},{1,29},{2,30},{3,31},{4,8},{5,9},{6,10},{7,11},{8,4},{9,5},... | collective-permute-start | bytes 638984 | tf_op jit(solution)/shard_map/ppermute | solution.py:41
  113.5 7.1 %collective-permute-start.31 = (f32[416,128]{1,0:T(8,128)S(1)}, f32[416,128]{1,0:T(8,128)S(1)}, u32[]{:S(2)}, u32[]{:S(2)}) collective-permute-start(f32[416,128]{1,0:T(8,128)S(1)} %get-tuple-element.46), channel_id=1, source_target_pairs={{0,4},{1,5},{2,6},{3,7},{4,0},{5,1},{6,2},{7,3},{8,12},{9,13},{10,... | collective-permute-start | bytes 638984 | tf_op jit(solution)/shard_map/ppermute | solution.py:41
  113.6 8.6 %collective-permute-start.32 = (f32[416,128]{1,0:T(8,128)S(1)}, f32[416,128]{1,0:T(8,128)S(1)}, u32[]{:S(2)}, u32[]{:S(2)}) collective-permute-start(f32[416,128]{1,0:T(8,128)S(1)} %get-tuple-element.47), channel_id=1, source_target_pairs={{0,28},{1,29},{2,30},{3,31},{4,8},{5,9},{6,10},{7,11},{8,4},{9,5},... | collective-permute-start | bytes 638984 | tf_op jit(solution)/shard_map/ppermute | solution.py:41
  122.5 5.2 %collective-permute-start.41 = (bf16[64,832]{1,0:T(8,128)(2,1)S(1)}, bf16[64,832]{1,0:T(8,128)(2,1)S(1)}, u32[]{:S(2)}, u32[]{:S(2)}) collective-permute-start(bf16[64,832]{1,0:T(8,128)(2,1)S(1)} %dynamic-slice_bitcast_fusion), channel_id=1, source_target_pairs={{0,2},{1,3},{2,0},{3,1},{4,6},{5,7},{6,4},{7,5},{8,10},{9,11},{10,... | collective-permute-start | bytes 319496 | tf_op jit(solution)/shard_map/ppermute | solution.py:21
  127.8 3.7 %collective-permute-start.42 = (bf16[2,32,832]{2,1,0:T(8,128)(2,1)S(1)}, bf16[2,32,832]{2,1,0:T(8,128)(2,1)S(1)}, u32[]{:S(2)}, u32[]{:S(2)}) collective-permute-start(bf16[2,32,832]{2,1,0:T(8,128)(2,1)S(1)} %fusion.1), channel_id=1, source_target_pairs={{0,1},{1,0},{2,3},{3,2},{4,5},{5,4},{6,7},{7,6},{8,9},{9,8},{10,11... | collective-permute-start | bytes 319496 | tf_op jit(solution)/shard_map/ppermute | solution.py:21
